TPU v7x, 128 devices: a whole 4x4x4 slice. The times are simulated.
128 devices in a mesh: rows: 16 (over z, y_hi, core), seq: 8 (over y_lo, x).
Axes of the slice: x: 4, y: 4 (y_hi: 2, y_lo: 2; y = y_hi * 2 + y_lo), z: 4, core: 2. Of those that a mesh axis runs over, the one named last changes fastest.
Arguments:
- inputs: bfloat16 [32, 1024, 768], P('rows', 'seq'), may hold values from -6 to 6
- lengths: int32 [32], P('rows'), may hold values from 128 to 1024, as said below
- qkv_weight: float32 [768, 3, 768], P(('rows', 'seq')), may hold values from -0.3125 to 0.3125
- out_weight: float32 [768, 768], P(('rows', 'seq')), may hold values from -0.875 to 0.875
- up_weight: float32 [768, 3072], P(('rows', 'seq')), may hold values from -0.21875 to 0.21875
- down_weight: float32 [3072, 768], P(('rows', 'seq')), may hold values from -0.21875 to 0.21875
- ln1_gain: float32 [768], P(('rows', 'seq')), may hold values from 0.25 to 1.75
- ln1_bias: float32 [768], P(('rows', 'seq')), may hold values from -1.5 to 1.5
- ln2_gain: float32 [768], P(('rows', 'seq')), may hold values from 0.25 to 1.75
- ln2_bias: float32 [768], P(('rows', 'seq')), may hold values from -1.5 to 1.5
- cotangent: bfloat16 [32, 1024, 768], P('rows', 'seq'), may hold values from -6 to 6
Outputs:
- output: bfloat16 [32, 1024, 768], P('rows', 'seq')
- input_grad: float32 [32, 1024, 768], P('rows', 'seq')
- qkv_grad: float32 [768, 3, 768], P(('rows', 'seq'))
- out_grad: float32 [768, 768], P(('rows', 'seq'))
- up_grad: float32 [768, 3072], P(('rows', 'seq'))
- down_grad: float32 [3072, 768], P(('rows', 'seq'))
- ln1_gain_grad: float32 [768], P(('rows', 'seq'))
- ln1_bias_grad: float32 [768], P(('rows', 'seq'))
- ln2_gain_grad: float32 [768], P(('rows', 'seq'))
- ln2_bias_grad: float32 [768], P(('rows', 'seq'))
Inputs may be any that keep to these rules, and one draw needn't show every extreme that they name: `lengths`: each row's count of valid tokens: keys at or past it are padding; in every draw one row holds exactly 1024 and another exactly 128.
All inputs are finite; a program needn't handle non-finite values.
Results may differ from a plain program's by a relative error of at most 0.017.
The roundings to bfloat16 on the way count: a program that leaves them out, or rounds other values in their place, can miss the bound.
Values may be sent and summed in bfloat16 or wider, within the bound.
A program may use at most 128 MiB of HBM per device.

v0:
```python
import functools
import math

import jax
import jax.numpy as jnp
import numpy as np
from jax import lax
from jax.experimental import pallas as pl
from jax.experimental.pallas import tpu as pltpu
from jax.sharding import PartitionSpec as P

MESH = pl.DeviceIdType.MESH
BF = jnp.bfloat16
F32 = jnp.float32
HEAD_DIM = 32
EPS = 1e-05
ROWS_A = 208
ROWS_B = 384
VM = pl.BlockSpec(memory_space=pltpu.VMEM)
SM = pl.BlockSpec(memory_space=pltpu.SMEM)


def perm_a():
    m = np.zeros((ROWS_A, 256), np.float32)
    for c in range(4):
        for s in range(8):
            for i in range(6):
                m[c * 48 + s * 6 + i, s * 32 + c * 6 + i] = 1
    for s in range(8):
        m[192 + s, s * 32 + 24] = 1
    return m


def perm_b():
    m = np.zeros((ROWS_B, 384), np.float32)
    for s in range(8):
        for j in range(4):
            for i in range(6):
                m[j * 48 + s * 6 + i, s * 48 + j * 6 + i] = 1
        for i in range(24):
            m[192 + s * 24 + i, s * 48 + 24 + i] = 1
    return m


def spread_m():
    m = np.zeros((256, 768), np.float32)
    for r in range(16):
        for s in range(8):
            m[r * 16 + s, (r * 8 + s) * 6 : (r * 8 + s) * 6 + 6] = 1
    return m


def spread_e():
    m = np.zeros((128, 768), np.float32)
    for j in range(768):
        m[j % 6, j] = 1
    return m


def const(m):
    return jnp.asarray(m, BF)


def nn(a, b):
    return lax.dot_general(a, b, (((1,), (0,)), ((), ())), preferred_element_type=F32)


def nt(a, b):
    return lax.dot_general(a, b, (((1,), (1,)), ((), ())), preferred_element_type=F32)


def tn(a, b):
    return lax.dot_general(a, b, (((0,), (0,)), ((), ())), preferred_element_type=F32)


class Place:
    def __init__(self):
        self.r = lax.axis_index("rows")
        self.s = lax.axis_index("seq")
        self.z = self.r // 4
        self.y = (self.r // 2) % 2
        self.c = self.r % 2

    def slot(self, dz, dy, dc):
        z = (self.z + dz) % 4
        y = (self.y + dy) % 2
        c = (self.c + dc) % 2
        return z * 4 + y * 2 + c

    def row_dev(self, dz, dy, dc):
        return {"rows": self.slot(dz, dy, dc)}

    def seq_at(self, d):
        return (self.s + d) % 8

    def seq_dev(self, d):
        return {"seq": self.seq_at(d)}


ROW_PEERS = ((0, 0, 1), (0, 1, 0), (1, 0, 0), (3, 0, 0))


def barrier(me):
    sem = pltpu.get_barrier_semaphore()
    for p in ROW_PEERS:
        pl.semaphore_signal(sem, inc=1, device_id=me.row_dev(*p), device_id_type=MESH)
    for d in range(1, 8):
        pl.semaphore_signal(sem, inc=1, device_id=me.seq_dev(d), device_id_type=MESH)
    pl.semaphore_wait(sem, len(ROW_PEERS) + 7)


def remote(src, dst, ss, rs, dev):
    return pltpu.make_async_remote_copy(
        src_ref=src, dst_ref=dst, send_sem=ss, recv_sem=rs, device_id=dev, device_id_type=MESH
    )


class Exchange:
    def __init__(self, me, src, dst, land, ss, rs, base):
        self.me, self.src, self.dst, self.land = me, src, dst, land
        self.ss, self.rs, self.base = ss, rs, base

    def _copy(self, d):
        return remote(
            self.src(d),
            self.dst(d),
            self.ss.at[self.base + d - 1],
            self.rs.at[self.base + d - 1],
            self.me.seq_dev(d),
        )

    def start(self):
        for d in range(1, 8):
            self._copy(d).start()

    def wait_recv(self):
        for d in range(1, 8):
            here = self.land(d)
            remote(
                here, here, self.ss.at[self.base + d - 1], self.rs.at[self.base + d - 1], self.me.seq_dev(d)
            ).wait_recv()

    def wait_send(self):
        for d in range(1, 8):
            self._copy(d).wait_send()


GATHER_SEMS = 17


class RowsGather:
    def __init__(self, me, buf, cut, ss, rs, base):
        self.me, self.buf, self.cut = me, buf, cut
        self.ss, self.rs, self.base = ss, rs, base
        self.sent = []

    def _part(self, rel, part):
        slot = self.me.slot(*rel)
        full = self.buf.shape[1]
        if part == 0:
            return self.buf.at[slot]
        if part == 1:
            return self.buf.at[slot, pl.ds(0, self.cut)]
        return self.buf.at[slot, pl.ds(self.cut, full - self.cut)]

    PLAN = {
        "y": (0, (0, 1, 0), (0, 0, 0), 0),
        "p0": (1, (1, 0, 0), (0, 0, 0), 0),
        "m0": (2, (3, 0, 0), (0, 0, 0), 0),
        "p1": (3, (1, 0, 0), (0, 1, 0), 0),
        "m1": (4, (3, 0, 0), (0, 1, 0), 0),
        "fp0": (5, (1, 0, 0), (3, 0, 0), 1),
        "fm0": (6, (3, 0, 0), (1, 0, 0), 2),
        "fp1": (7, (1, 0, 0), (3, 1, 0), 1),
        "fm1": (8, (3, 0, 0), (1, 1, 0), 2),
        "c00": (9, (0, 0, 1), (0, 0, 0), 0),
        "c01": (10, (0, 0, 1), (0, 1, 0), 0),
        "c10": (11, (0, 0, 1), (1, 0, 0), 0),
        "c11": (12, (0, 0, 1), (1, 1, 0), 0),
        "c20": (13, (0, 0, 1), (2, 0, 0), 0),
        "c21": (14, (0, 0, 1), (2, 1, 0), 0),
        "c30": (15, (0, 0, 1), (3, 0, 0), 0),
        "c31": (16, (0, 0, 1), (3, 1, 0), 0),
    }

    def _send(self, name):
        i, to, block, part = self.PLAN[name]
        ref = self._part(block, part)
        return remote(ref, ref, self.ss.at[self.base + i], self.rs.at[self.base + i], self.me.row_dev(*to))

    def send(self, *names):
        for name in names:
            self._send(name).start()
            self.sent.append(name)

    def recv(self, *names):
        for name in names:
            i, to, block, part = self.PLAN[name]
            rel = ((block[0] - to[0]) % 4, (block[1] - to[1]) % 2, (block[2] - to[2]) % 2)
            ref = self._part(rel, part)
            remote(ref, ref, self.ss.at[self.base + i], self.rs.at[self.base + i], self.me.row_dev(*to)).wait_recv()

    def step0(self):
        self.send("y", "p0", "m0", "c00")

    def step1(self):
        self.recv("y")
        self.send("p1", "m1", "c01")

    def step2(self):
        self.recv("p0")
        self.send("fp0", "c30")
        self.recv("m0")
        self.send("fm0", "c10")

    def step3(self):
        self.recv("p1")
        self.send("fp1", "c31")
        self.recv("m1")
        self.send("fm1", "c11")

    def step4(self):
        self.recv("fp0", "fm0")
        self.send("c20")

    def step5(self):
        self.recv("fp1", "fm1")
        self.send("c21")

    def step6(self):
        self.recv("c00", "c01", "c10", "c11", "c20", "c21", "c30", "c31")

    def finish(self):
        for name in self.sent:
            self._send(name).wait_send()

    def steps(self):
        return [self.step0, self.step1, self.step2, self.step3, self.step4, self.step5, self.step6]


SCATTER_SEMS = 15


class RowsScatter:
    def __init__(self, me, g, cr, zlo, zhi, zr, yr, cut, ss, rs, base):
        self.me, self.g, self.cr, self.zlo, self.zhi, self.zr, self.yr = me, g, cr, zlo, zhi, zr, yr
        self.cut, self.ss, self.rs, self.base = cut, ss, rs, base
        self.full = g.shape[1]
        self.open = []

    def _copy(self, i, src, dst, to):
        return remote(src, dst, self.ss.at[self.base + i], self.rs.at[self.base + i], self.me.row_dev(*to))

    def _start(self, i, src, dst, to):
        copy = self._copy(i, src, dst, to)
        copy.start()
        self.open.append(copy)

    def _landed(self, i, dst, to):
        self._copy(i, dst, dst, to).wait_recv()

    ORDER = ((2, 0), (2, 1), (1, 0), (1, 1), (3, 0), (3, 1), (0, 1), (0, 0))

    def start_core(self, which=None):
        for k, (dz, dy) in enumerate(self.ORDER):
            self._start(k, self.g.at[self.me.slot(dz, dy, 1)], self.cr.at[k], (0, 0, 1))

    def _add(self, k):
        dz, dy = self.ORDER[k]
        self._landed(k, self.cr.at[k], (0, 0, 1))
        slot = self.me.slot(dz, dy, 0)
        self.g[slot] = (self.g[slot].astype(F32) + self.cr[k].astype(F32)).astype(BF)

    def add_far(self):
        lo, hi = pl.ds(0, self.cut), pl.ds(self.cut, self.full - self.cut)
        for dy in (0, 1):
            self._add(dy)
            slot = self.me.slot(2, dy, 0)
            self._start(8 + dy, self.g.at[slot, lo], self.zlo.at[dy], (1, 0, 0))
            self._start(10 + dy, self.g.at[slot, hi], self.zhi.at[dy], (3, 0, 0))

    def add_near(self):
        for k in (2, 3, 4, 5):
            self._add(k)

    def pass_near(self):
        lo, hi = pl.ds(0, self.cut), pl.ds(self.cut, self.full - self.cut)
        for dy in (0, 1):
            self._landed(8 + dy, self.zlo.at[dy], (1, 0, 0))
            slot = self.me.slot(1, dy, 0)
            self.g[slot, lo] = (self.g[slot, lo].astype(F32) + self.zlo[dy].astype(F32)).astype(BF)
            self._landed(10 + dy, self.zhi.at[dy], (3, 0, 0))
            slot = self.me.slot(3, dy, 0)
            self.g[slot, hi] = (self.g[slot, hi].astype(F32) + self.zhi[dy].astype(F32)).astype(BF)
        both = self.me.y == 0
        p0, p1 = self.me.slot(1, 0, 0), self.me.slot(1, 1, 0)
        m0, m1 = self.me.slot(3, 0, 0), self.me.slot(3, 1, 0)
        self._start(12, self.g.at[p1], self.zr.at[0, 1], (1, 0, 0))
        self._start(13, self.g.at[m1], self.zr.at[1, 1], (3, 0, 0))
        self._start(14, self.g.at[p0], self.zr.at[0, 0], (1, 0, 0))
        self._start(15, self.g.at[m0], self.zr.at[1, 0], (3, 0, 0))

    def own_core(self):
        self._add(6)
        self._add(7)

    def cross(self):
        self._landed(12, self.zr.at[0, 1], (1, 0, 0))
        self._landed(13, self.zr.at[1, 1], (3, 0, 0))
        slot = self.me.slot(0, 1, 0)
        total = self.g[slot].astype(F32) + self.zr[0, 1].astype(F32) + self.zr[1, 1].astype(F32)
        self.g[slot] = total.astype(BF)
        self._start(16, self.g.at[slot], self.yr, (0, 1, 0))

    def last(self):
        self._landed(14, self.zr.at[0, 0], (1, 0, 0))
        self._landed(15, self.zr.at[1, 0], (3, 0, 0))
        self._landed(16, self.yr, (0, 1, 0))
        slot = self.me.slot(0, 0, 0)
        return (
            self.g[slot].astype(F32)
            + self.zr[0, 0].astype(F32)
            + self.zr[1, 0].astype(F32)
            + self.yr[...].astype(F32)
        )

    def finish(self):
        for copy in self.open:
            copy.wait_send()


SCATTER_SEMS = 17


def small_vec(ref, row):
    lane = lax.broadcasted_iota(jnp.int32, (1, 128), 1)
    out = jnp.zeros((1, 128), F32)
    for i in range(6):
        out = jnp.where(lane == i, ref[i], out)
    return out


def normalise(v):
    mean = jnp.mean(v, axis=-1, keepdims=True)
    centred = v - mean
    var = jnp.mean(centred * centred, axis=-1, keepdims=True)
    inverse = lax.rsqrt(var + EPS)
    return centred * inverse, inverse


SCALE = HEAD_DIM**-0.5
LOG2E = 1.4426950408889634
BASE = (0, 256, 768, 1536)


def lanes(ref, b, c, h, first, count):
    rows = pl.ds(pl.multiple_of(h * 32, 32), 32)
    if c is None:
        parts = [ref[b, first + i, rows, :] for i in range(count)]
    else:
        parts = [ref[b, first + i, c, rows, :] for i in range(count)]
    return parts[0] if count == 1 else jnp.concatenate(parts, axis=1)


def allowed(nk, length):
    key = lax.broadcasted_iota(jnp.int32, (nk, 256), 0)
    query = lax.broadcasted_iota(jnp.int32, (nk, 256), 1) + (nk - 256)
    return (key <= query) & (key < length)


def attend_one(heads_ref, length, p_ref, l_ref, os_ref, b, h, i):
    rows = pl.ds(pl.multiple_of(h * 32, 32), 32)
    kt = lanes(heads_ref, b, 1, h, 0, 8)
    vt = lanes(heads_ref, b, 2, h, 0, 8)
    for qb in range(4):
        nk = (qb + 1) * 256
        qt = lanes(heads_ref, b, 0, h, 2 * qb, 2)
        s = tn(kt[:, :nk], qt)
        s = jnp.where(allowed(nk, length), s, -1e30)
        top = jnp.max(s, axis=0, keepdims=True)
        p = jnp.exp2((s - top) * (SCALE * LOG2E))
        inverse = 1.0 / jnp.sum(p, axis=0, keepdims=True)
        low = p.astype(BF)
        p_ref[i, pl.ds(BASE[qb], nk), :] = low
        l_ref[i, pl.ds(qb, 1), :] = inverse
        o = (nn(vt[:, :nk], low) * inverse).astype(BF)
        os_ref[b, 2 * qb, rows, :] = o[:, :128]
        os_ref[b, 2 * qb + 1, rows, :] = o[:, 128:]


def attend_one_back(heads_ref, p_ref, l_ref, os_ref, do_ref, dq_ref, acc_ref, b, h, i):
    rows = pl.ds(pl.multiple_of(h * 32, 32), 32)
    kt = lanes(heads_ref, b, 1, h, 0, 8)
    vt = lanes(heads_ref, b, 2, h, 0, 8)
    for qb in range(4):
        nk = (qb + 1) * 256
        qt = lanes(heads_ref, b, 0, h, 2 * qb, 2)
        do = lanes(do_ref, b, None, h, 2 * qb, 2).astype(F32) * l_ref[i, pl.ds(qb, 1), :]
        o = lanes(os_ref, b, None, h, 2 * qb, 2).astype(F32)
        delta = jnp.sum(do * o, axis=0, keepdims=True)
        low = do.astype(BF)
        p = p_ref[i, pl.ds(BASE[qb], nk), :]
        ds = (p.astype(F32) * (tn(vt[:, :nk], low) - delta)).astype(BF)
        dv = nt(low, p)
        dk = nt(qt, ds)
        if nk > 256:
            acc_ref[0, :, : nk - 256] += dk[:, : nk - 256]
            acc_ref[1, :, : nk - 256] += dv[:, : nk - 256]
        acc_ref[0, :, nk - 256 : nk] = dk[:, nk - 256 :]
        acc_ref[1, :, nk - 256 : nk] = dv[:, nk - 256 :]
        dq = (nn(kt[:, :nk], ds) * SCALE).astype(BF)
        dq_ref[b, 2 * qb, 0, rows, :] = dq[:, :128]
        dq_ref[b, 2 * qb + 1, 0, rows, :] = dq[:, 128:]
    for j in range(8):
        dq_ref[b, j, 1, rows, :] = (acc_ref[0, :, j * 128 : (j + 1) * 128] * SCALE).astype(BF)
        dq_ref[b, j, 2, rows, :] = acc_ref[1, :, j * 128 : (j + 1) * 128].astype(BF)


def feed_forward(gb_ref, h2_ref, dy_ref, y_ref, dh_ref):
    dh_ref[...] = jnp.zeros_like(dh_ref)

    def block(j, carry):
        up = pl.ds(pl.multiple_of(j * 48, 16), 48)
        deep = pl.ds(j * 4, 4)
        wu = gb_ref[:, up, :].reshape(768, 768)
        h2 = h2_ref[...]
        u = nn(h2, wu)
        phi = 0.5 + 0.5 * lax.erf(u * (1.0 / math.sqrt(2.0)))
        act = (u * phi).astype(BF)
        slope = phi + u * jnp.exp(-0.5 * u * u) * (1.0 / math.sqrt(2.0 * math.pi))
        wd = gb_ref[deep, pl.ds(192, 192), :].reshape(768, 768)
        dy = dy_ref[...].reshape(256, 768)
        y_ref[...] += nn(act, wd)
        du = (nt(dy, wd) * slope).astype(BF)
        gb_ref[deep, pl.ds(192, 192), :] = tn(act, dy).astype(BF).reshape(4, 192, 768)
        dh_ref[...] += nt(du, wu)
        gb_ref[:, up, :] = tn(h2, du).astype(BF).reshape(16, 48, 768)
        return carry

    lax.fori_loop(0, 4, block, 0)


def norm_parts(grad, gain, scaled, inverse):
    weighted = grad * gain
    first = jnp.mean(weighted, axis=-1, keepdims=True)
    second = jnp.mean(weighted * scaled, axis=-1, keepdims=True)
    grad_in = inverse * (weighted - first - scaled * second)
    return grad_in, jnp.sum(grad * scaled, axis=0, keepdims=True), jnp.sum(grad, axis=0, keepdims=True)


HBM = pl.BlockSpec(memory_space=pl.ANY)


class Counter:
    def __init__(self):
        self.n = 0

    def take(self, k):
        first = self.n
        self.n += k
        return first


def plan():
    c = Counter()
    at = {"xa": c.take(7), "xb": c.take(7), "ga": c.take(GATHER_SEMS), "gb": c.take(GATHER_SEMS)}
    for name in ("q", "o", "do", "dq"):
        at[name] = c.take(14)
    at["ra"] = c.take(SCATTER_SEMS)
    at["rb"] = c.take(SCATTER_SEMS)
    at["sa"] = c.take(7)
    at["sb"] = c.take(7)
    return at, c.n


def scatter_scratch(rows, cut):
    return [
        pltpu.VMEM((8, rows, 768), BF),
        pltpu.VMEM((2, cut, 768), BF),
        pltpu.VMEM((2, rows - cut, 768), BF),
        pltpu.VMEM((2, 2, rows, 768), BF),
        pltpu.VMEM((rows, 768), BF),
    ]


SCRATCH = dict(
    x=pltpu.VMEM((2, 128, 768), BF),
    dy=pltpu.VMEM((2, 128, 768), BF),
    wq=pltpu.VMEM((6, 3, 768), F32),
    wo=pltpu.VMEM((6, 768), F32),
    wu=pltpu.VMEM((6, 3072), F32),
    wd=pltpu.VMEM((24, 768), F32),
    pa=pltpu.VMEM((ROWS_A, 256), BF),
    pb=pltpu.VMEM((ROWS_B, 384), BF),
    sm=pltpu.VMEM((256, 768), BF),
    se=pltpu.VMEM((128, 768), BF),
    f=pltpu.VMEM((80, 768), F32),
    ka=pltpu.VMEM((32, 768), BF),
    kb=pltpu.VMEM((48, 768), BF),
    xa=pltpu.VMEM((8, 32, 768), BF),
    xb=pltpu.VMEM((8, 48, 768), BF),
    ga=pltpu.VMEM((16, ROWS_A, 768), BF),
    gb=pltpu.VMEM((16, ROWS_B, 768), BF),
    lnp=pltpu.VMEM((8, 768), F32),
    xhat=pltpu.VMEM((256, 768), F32),
    inv=pltpu.VMEM((256, 1), F32),
    h1=pltpu.VMEM((256, 768), BF),
    sq=pltpu.VMEM((8, 2, 3, 96, 128), BF),
    heads=pltpu.VMEM((2, 8, 3, 96, 128), BF),
    p=pltpu.VMEM((6, 2560, 256), BF),
    l=pltpu.VMEM((6, 4, 256), F32),
    os=pltpu.VMEM((2, 8, 96, 128), BF),
    ot=pltpu.VMEM((2, 8, 96, 128), BF),
    h2=pltpu.VMEM((256, 768), BF),
    xh2=pltpu.VMEM((256, 768), F32),
    y=pltpu.VMEM((256, 768), F32),
    dh=pltpu.VMEM((256, 768), F32),
    dx=pltpu.VMEM((256, 768), F32),
    dot=pltpu.VMEM((2, 8, 96, 128), BF),
    do=pltpu.VMEM((2, 8, 96, 128), BF),
    acc=pltpu.VMEM((2, 32, 1024), F32),
    dq=pltpu.VMEM((2, 8, 3, 96, 128), BF),
    dqt=pltpu.VMEM((2, 8, 3, 96, 128), BF),
    outv=pltpu.VMEM((2, 128, 768), BF),
    pka=pltpu.VMEM((8, 32, 768), BF),
    pkb=pltpu.VMEM((8, 48, 768), BF),
    xsa=pltpu.VMEM((8, 32, 768), BF),
    xsb=pltpu.VMEM((8, 48, 768), BF),
)


def feature_major(ref, b):
    return ref[b].reshape(768, 128)


def layer_kernel(*refs):
    (x_in, wq_in, wo_in, wu_in, wd_in, dy_in, pa_in, pb_in, sm_in, se_in, len_ref, g1_ref, b1_ref, g2_ref, b2_ref) = refs[:15]
    out_ref, ig_ref, sum_ref = refs[15:18]
    names = list(SCRATCH)
    v = dict(zip(names, refs[18 : 18 + len(names)]))
    rest = refs[18 + len(names) :]
    scr_a, scr_b = rest[:5], rest[5:10]
    ss, rs, ls = rest[10:]
    at, _ = plan()
    me = Place()

    loads = {}
    for i, (name, src) in enumerate(
        (("wq", wq_in), ("wo", wo_in), ("wu", wu_in), ("wd", wd_in), ("pa", pa_in), ("x", x_in), ("pb", pb_in),
         ("sm", sm_in), ("se", se_in), ("dy", dy_in))
    ):
        loads[name] = pltpu.make_async_copy(src, v[name], ls.at[i])
        loads[name].start()

    f = v["f"]
    f[pl.ds(24, 8), :] = jnp.zeros((8, 768), F32)
    for p, ref in enumerate((g1_ref, b1_ref, g2_ref, b2_ref)):
        f[pl.ds(24, 1), pl.ds(p * 128, 128)] = small_vec(ref, p)
    for name in ("wq", "wo", "wu", "wd"):
        loads[name].wait()
    for c in range(3):
        for i in range(6):
            f[pl.ds(c * 6 + i, 1), :] = v["wq"][i, pl.ds(c, 1), :]
    f[pl.ds(18, 6), :] = v["wo"][...]
    v["ka"][...] = f[pl.ds(0, 32), :].astype(BF)
    for j in range(4):
        f[pl.ds(32 + j * 6, 6), :] = v["wu"][:, pl.ds(j * 768, 768)]
    f[pl.ds(56, 24), :] = v["wd"][...]
    v["kb"][...] = f[pl.ds(32, 48), :].astype(BF)
    barrier(me)

    def seq_gather(src, dst, key):
        return Exchange(me, lambda d: src, lambda d: dst.at[me.s], lambda d: dst.at[me.seq_at(8 - d)], ss, rs, at[key])

    def by_row(src, dst, key, flip=False):
        made = []
        for b in range(2):
            if flip:
                out = lambda d, b=b: src.at[me.seq_at(d), b]
            else:
                out = lambda d, b=b: src.at[b, me.seq_at(d)]
            made.append(
                Exchange(me, out, lambda d, b=b: dst.at[b, me.s], lambda d, b=b: dst.at[b, me.seq_at(8 - d)], ss, rs, at[key] + 7 * b)
            )
        return made

    x_a = seq_gather(v["ka"], v["xa"], "xa")
    x_b = seq_gather(v["kb"], v["xb"], "xb")
    x_a.start()
    x_b.start()
    v["xa"][me.s] = v["ka"][...]
    v["xb"][me.s] = v["kb"][...]
    loads["x"].wait()
    xhat, inverse = normalise(v["x"][...].reshape(256, 768).astype(F32))
    v["xhat"][...] = xhat
    v["inv"][...] = inverse
    for name in ("pa", "pb", "sm", "se", "dy"):
        loads[name].wait()

    ga, gb = v["ga"], v["gb"]
    ag_a = RowsGather(me, ga, 112, ss, rs, at["ga"])
    ag_b = RowsGather(me, gb, 192, ss, rs, at["gb"])
    x_a.wait_recv()
    ga[me.r] = nn(v["pa"][...], v["xa"][...].reshape(256, 768)).astype(BF)
    ag_a.step0()
    x_b.wait_recv()
    gb[me.r] = nn(v["pb"][...], v["xb"][...].reshape(384, 768)).astype(BF)
    ag_a.step1()
    ag_a.step2()
    ag_a.step3()
    ag_b.step0()
    ag_a.step4()
    ag_a.step5()
    ag_a.step6()

    lnp = v["lnp"]
    ln = ga[:, pl.ds(192, 16), :].reshape(256, 768)
    for p in range(4):
        spread = nn(ln[:, p * 128 : (p + 1) * 128], v["se"][...])
        lnp[pl.ds(p, 1), :] = jnp.sum(spread * v["sm"][...].astype(F32), axis=0, keepdims=True)
    h1 = (v["xhat"][...] * lnp[pl.ds(0, 1), :] + lnp[pl.ds(1, 1), :]).astype(BF)
    v["h1"][...] = h1
    for c in range(3):
        w = ga[:, pl.ds(c * 48, 48), :].reshape(768, 768)
        val = nn(h1, w).T.astype(BF)
        for k in range(8):
            for b in range(2):
                v["sq"][k, b, c] = val[k * 96 : (k + 1) * 96, b * 128 : (b + 1) * 128]
    x_q = by_row(v["sq"], v["heads"], "q", flip=True)
    for b in range(2):
        x_q[b].start()
        v["heads"][b, me.s] = v["sq"][me.s, b]
    ag_b.step1()

    x_o = by_row(v["os"], v["ot"], "o")

    def forward(b):
        x_q[b].wait_recv()

        def one(h, carry):
            attend_one(v["heads"], len_ref[b], v["p"], v["l"], v["os"], b, h, b * 3 + h)
            return carry

        lax.fori_loop(0, 3, one, 0)
        x_o[b].start()
        v["ot"][b, me.s] = v["os"][b, me.s]

    forward(0)
    ag_b.step2()
    forward(1)
    ag_b.step3()
    ag_b.step4()
    ag_b.step5()

    for b in range(2):
        x_o[b].wait_recv()
    ot = jnp.concatenate([feature_major(v["ot"], b) for b in range(2)], axis=1)
    wo = ga[:, pl.ds(144, 48), :].reshape(768, 768)
    x1 = v["x"][...].reshape(256, 768).astype(F32) + tn(ot, wo)
    xhat2, inverse2 = normalise(x1)
    v["xh2"][...] = xhat2
    v["h2"][...] = (xhat2 * lnp[pl.ds(2, 1), :] + lnp[pl.ds(3, 1), :]).astype(BF)
    v["y"][...] = x1
    ag_b.step6()
    ag_b.finish()
    ag_a.finish()

    feed_forward(gb, v["h2"], v["dy"], v["y"], v["dh"])
    rs_b = RowsScatter(me, gb, *scr_b, 192, ss, rs, at["rb"])
    rs_b.start_core()

    v["outv"][...] = v["y"][...].astype(BF).reshape(2, 128, 768)
    store_out = pltpu.make_async_copy(v["outv"], out_ref, ls.at[10])
    store_out.start()
    grad_in, gg2, gb2 = norm_parts(v["dh"][...], lnp[pl.ds(2, 1), :], v["xh2"][...], inverse2)
    dx = v["dy"][...].reshape(256, 768).astype(F32) + grad_in
    v["dx"][...] = dx
    low = dx.astype(BF)
    d = nt(wo, low).astype(BF)
    for k in range(8):
        for b in range(2):
            v["dot"][b, k] = d[k * 96 : (k + 1) * 96, b * 128 : (b + 1) * 128]
    x_do = by_row(v["dot"], v["do"], "do")
    for b in range(2):
        x_do[b].start()
        v["do"][b, me.s] = v["dot"][b, me.s]
    ga[:, pl.ds(144, 48), :] = nn(ot, low).astype(BF).reshape(16, 48, 768)
    rs_b.add_far()
    rs_b.add_near()

    x_dq = by_row(v["dq"], v["dqt"], "dq")

    def backward(b):
        x_do[b].wait_recv()

        def one(h, carry):
            attend_one_back(v["heads"], v["p"], v["l"], v["os"], v["do"], v["dq"], v["acc"], b, h, b * 3 + h)
            return carry

        lax.fori_loop(0, 3, one, 0)
        x_dq[b].start()
        v["dqt"][b, me.s] = v["dq"][b, me.s]

    backward(0)
    rs_b.pass_near()
    backward(1)
    rs_b.own_core()
    for b in range(2):
        x_dq[b].wait_recv()

    dh1 = jnp.zeros((256, 768), F32)
    for c in range(3):
        dqt = jnp.concatenate([v["dqt"][b, :, c].reshape(768, 128) for b in range(2)], axis=1)
        dq = dqt.T
        dh1 += nt(dq, ga[:, pl.ds(c * 48, 48), :].reshape(768, 768))
        ga[:, pl.ds(c * 48, 48), :] = tn(v["h1"][...], dq).astype(BF).reshape(16, 48, 768)
    grad_in, gg1, gb1 = norm_parts(dh1, lnp[pl.ds(0, 1), :], v["xhat"][...], v["inv"][...])
    ga[:, pl.ds(192, 16), pl.ds(512, 256)] = jnp.zeros((16, 16, 256), BF)
    for p, vec in enumerate((gg1, gb1, gg2, gb2)):
        rows = (v["sm"][...].astype(F32) * vec).astype(BF)
        ga[:, pl.ds(192, 16), pl.ds(p * 128, 128)] = nt(rows, v["se"][...]).astype(BF).reshape(16, 16, 128)
    rs_a = RowsScatter(me, ga, *scr_a, 112, ss, rs, at["ra"])
    rs_a.start_core()
    v["xhat"][...] = v["dx"][...] + grad_in
    store_ig = []
    for b in range(2):
        store_ig.append(pltpu.make_async_copy(v["xhat"].at[pl.ds(b * 128, 128)], ig_ref.at[b], ls.at[11 + b]))
        store_ig[b].start()
    rs_b.cross()
    rs_a.add_far()
    rs_a.add_near()
    total = rs_b.last().astype(BF)
    v["pkb"][...] = tn(v["pb"][...], total).astype(BF).reshape(8, 48, 768)

    def seq_scatter(src, dst, key):
        made = Exchange(
            me, lambda d: src.at[me.seq_at(d)], lambda d: dst.at[me.s], lambda d: dst.at[me.seq_at(8 - d)], ss, rs, at[key]
        )
        made.start()
        dst[me.s] = src[me.s]
        return made

    s_b = seq_scatter(v["pkb"], v["xsb"], "sb")
    rs_a.pass_near()
    rs_a.own_core()
    rs_a.cross()
    total = rs_a.last().astype(BF)
    v["pka"][...] = tn(v["pa"][...], total).astype(BF).reshape(8, 32, 768)
    s_a = seq_scatter(v["pka"], v["xsa"], "sa")
    s_b.wait_recv()
    f[pl.ds(32, 48), :] = jnp.sum(v["xsb"][...].astype(F32), axis=0)
    s_a.wait_recv()
    f[pl.ds(0, 32), :] = jnp.sum(v["xsa"][...].astype(F32), axis=0)
    store_f = pltpu.make_async_copy(f, sum_ref, ls.at[13])
    store_f.start()
    for each in (x_a, x_b, *x_q, *x_o, *x_do, *x_dq, s_a, s_b):
        each.wait_send()
    rs_a.finish()
    rs_b.finish()
    for store in (store_out, *store_ig, store_f):
        store.wait()


def final_kernel(out_in, ig_in, f_in, out_ref, ig_ref, dwq_ref, dwo_ref, dwu_ref, dwd_ref, ln_ref, out_v, ig_v, f_ref, sem):
    loads = [
        pltpu.make_async_copy(src, dst, sem.at[i])
        for i, (src, dst) in enumerate(((f_in, f_ref), (ig_in, ig_v), (out_in, out_v)))
    ]
    for load in loads:
        load.start()
    a = pltpu.make_async_copy(out_v, out_ref, sem.at[3])
    b = pltpu.make_async_copy(ig_v, ig_ref, sem.at[4])
    loads[1].wait()
    b.start()
    loads[2].wait()
    a.start()
    loads[0].wait()
    for c in range(3):
        for i in range(6):
            dwq_ref[i, pl.ds(c, 1), :] = f_ref[pl.ds(c * 6 + i, 1), :]
    dwo_ref[...] = f_ref[pl.ds(18, 6), :]
    ln_ref[...] = f_ref[pl.ds(24, 8), :]
    for j in range(4):
        dwu_ref[:, pl.ds(j * 768, 768)] = f_ref[pl.ds(32 + j * 6, 6), :]
    dwd_ref[...] = f_ref[pl.ds(56, 24), :]
    a.wait()
    b.wait()


def on_device(inputs, lengths, qkv_weight, out_weight, up_weight, down_weight, ln1_gain, ln1_bias, ln2_gain, ln2_bias, cotangent):
    sds = jax.ShapeDtypeStruct
    n = plan()[1]
    out, ig, sums = pl.pallas_call(
        layer_kernel,
        out_shape=(sds((2, 128, 768), BF), sds((2, 128, 768), F32), sds((80, 768), F32)),
        in_specs=[HBM] * 10 + [SM] * 5,
        out_specs=[HBM] * 3,
        scratch_shapes=[
            *SCRATCH.values(),
            *scatter_scratch(ROWS_A, 112),
            *scatter_scratch(ROWS_B, 192),
            pltpu.SemaphoreType.DMA((n,)),
            pltpu.SemaphoreType.DMA((n,)),
            pltpu.SemaphoreType.DMA((14,)),
        ],
        compiler_params=pltpu.CompilerParams(collective_id=0, has_side_effects=True, vmem_limit_bytes=60 * 1024 * 1024),
        name="layer",
    )(
        inputs, qkv_weight, out_weight, up_weight, down_weight, cotangent,
        const(perm_a()), const(perm_b()), const(spread_m()), const(spread_e()),
        lengths, ln1_gain, ln1_bias, ln2_gain, ln2_bias,
    )
    res = pl.pallas_call(
        final_kernel,
        out_shape=(
            sds((2, 128, 768), BF), sds((2, 128, 768), F32), sds((6, 3, 768), F32), sds((6, 768), F32),
            sds((6, 3072), F32), sds((24, 768), F32), sds((8, 768), F32),
        ),
        in_specs=[HBM] * 3,
        out_specs=[HBM, HBM] + [VM] * 5,
        scratch_shapes=[
            pltpu.VMEM((2, 128, 768), BF),
            pltpu.VMEM((2, 128, 768), F32),
            pltpu.VMEM((80, 768), F32),
            pltpu.SemaphoreType.DMA((5,)),
        ],
        name="final",
    )(out, ig, sums)
    return (*res[:6], *[res[6][0, p * 128 : p * 128 + 6] for p in range(4)])


def solution(mesh):
    both = ("rows", "seq")
    return jax.shard_map(
        on_device,
        mesh=mesh,
        in_specs=(P("rows", "seq", None), P("rows"), P(both, None, None), P(both, None), P(both, None), P(both, None),
                  P(both), P(both), P(both), P(both), P("rows", "seq", None)),
        out_specs=(P("rows", "seq", None), P("rows", "seq", None), P(both, None, None), P(both, None), P(both, None),
                   P(both, None), P(both), P(both), P(both), P(both)),
        check_vma=False,
    )
```

profile of v0, /device:TPU:0, one launch (start us, length us, event | category | flops | bytes accessed | tf_op | source)
XLA Modules:
  0.0 177.9 jit_solution(1936900348506750797)
XLA Ops:
  0.6 173.0 %layer.1 = (bf16[2,128,768]{2,1,0:T(8,128)(2,1)}, f32[2,128,768]{2,1,0:T(8,128)}, f32[80,768]{1,0:T(8,128)}) custom-call(bf16[2,128,768]{2,1,0:T(8,128)(2,1)} %refs_0_.1, f32[6,3,768]{2,1,0:T(4,128)} %refs_1_.1, f32[6,768]{1,0:T(8,128)} %refs_2_.1, f32[6,3072]{1,0:T(8,128)} %refs_3_.1, f32[24,768]{1,0:T(8,128)} %refs_4_.1, bf16[2,128,768]{2,1,0:T(8,128)(2,1)} %refs_5_.1, ...), custom_call_target="tpu_custom_call" | custom-call | tf_op jit(solution)/shard_map/layer/pallas_call | solution.py:793
  173.6 3.0 %final.1 = (bf16[2,128,768]{2,1,0:T(8,128)(2,1)}, f32[2,128,768]{2,1,0:T(8,128)}, f32[6,3,768]{2,1,0:T(4,128)}, f32[6,768]{1,0:T(8,128)}, f32[6,3072]{1,0:T(8,12...) custom-call(bf16[2,128,768]{2,1,0:T(8,128)(2,1)} %get-tuple-element.20.out_in, f32[2,128,768]{2,1,0:T(8,128)} %get-tuple-element.21.ig_in, ...), custom_call_target="tpu_custom_call" | custom-call | tf_op jit(solution)/shard_map/final/pallas_call | solution.py:813
  176.6 1.2 slice_bitcast_fusion
where the time goes:
time: 178 us
  Pallas kernels  176 us (99%)
    pallas_call x1, Pallas kernels, on_device(): pl.pallas_call(layer_kernel, out_shape=(sds((2, 128, 768), BF), sds((2, 1...  173 us

commit v1 on v0

v1 whole, which is shorter than its diff:
```python
import functools
import math

import jax
import jax.numpy as jnp
import numpy as np
from jax import lax
from jax.experimental import pallas as pl
from jax.experimental.pallas import tpu as pltpu
from jax.sharding import PartitionSpec as P

MESH = pl.DeviceIdType.MESH
BF = jnp.bfloat16
F32 = jnp.float32
HEAD_DIM = 32
EPS = 1e-05
ROWS_A = 160
ROWS_U = 240
ROWS_W = 192
VM = pl.BlockSpec(memory_space=pltpu.VMEM)
SM = pl.BlockSpec(memory_space=pltpu.SMEM)


def perm_a():
    m = np.zeros((ROWS_A, 256), np.float32)
    for s in range(8):
        for c in range(3):
            for i in range(6):
                m[c * 48 + s * 6 + i, s * 32 + c * 6 + i] = 1
        m[144 + s, s * 32 + 18] = 1
    return m


def perm_u():
    m = np.zeros((ROWS_U, 256), np.float32)
    for s in range(8):
        for j in range(5):
            for i in range(6):
                m[j * 48 + s * 6 + i, s * 32 + j * 6 + i] = 1
    return m


def perm_w():
    m = np.zeros((ROWS_W, 256), np.float32)
    for s in range(8):
        for i in range(24):
            m[s * 24 + i, s * 32 + i] = 1
    return m


def spread_m():
    m = np.zeros((256, 768), np.float32)
    for r in range(16):
        for s in range(8):
            m[r * 16 + s, (r * 8 + s) * 6 : (r * 8 + s) * 6 + 6] = 1
    return m


def spread_e():
    m = np.zeros((4, 128, 768), np.float32)
    for p in range(4):
        for j in range(768):
            m[p, p * 32 + j % 6, j] = 1
    return m


def groups_e():
    m = np.zeros((768, 1024), np.float32)
    for j in range(768):
        m[j, j // 96 * 128 + j % 96] = 1
    return m


def const(m):
    return jnp.asarray(m, BF)


def nn(a, b):
    return lax.dot_general(a, b, (((1,), (0,)), ((), ())), preferred_element_type=F32)


def nt(a, b):
    return lax.dot_general(a, b, (((1,), (1,)), ((), ())), preferred_element_type=F32)


def tn(a, b):
    return lax.dot_general(a, b, (((0,), (0,)), ((), ())), preferred_element_type=F32)


class Place:
    def __init__(self):
        self.r = lax.axis_index("rows")
        self.s = lax.axis_index("seq")
        self.z = self.r // 4
        self.y = (self.r // 2) % 2
        self.c = self.r % 2

    def slot(self, dz, dy, dc):
        z = (self.z + dz) % 4
        y = (self.y + dy) % 2
        c = (self.c + dc) % 2
        return z * 4 + y * 2 + c

    def row_dev(self, dz, dy, dc):
        return {"rows": self.slot(dz, dy, dc)}

    def along_seq(self):
        return SeqPlace(self.s)

    def seq_at(self, d):
        return (self.s + d) % 8

    def seq_dev(self, d):
        return {"seq": self.seq_at(d)}


class SeqPlace:
    def __init__(self, s):
        self.s = s

    def slot(self, dx, dy, dc):
        return (self.s // 4 + dy) % 2 * 4 + (self.s + dx) % 4

    def row_dev(self, dx, dy, dc):
        return {"seq": self.slot(dx, dy, dc)}


ROW_PEERS = ((0, 0, 1), (0, 1, 0), (1, 0, 0), (3, 0, 0))


def barrier_signal(me):
    sem = pltpu.get_barrier_semaphore()
    for p in ROW_PEERS:
        pl.semaphore_signal(sem, inc=1, device_id=me.row_dev(*p), device_id_type=MESH)
    for d in range(1, 8):
        pl.semaphore_signal(sem, inc=1, device_id=me.seq_dev(d), device_id_type=MESH)


def barrier_wait():
    pl.semaphore_wait(pltpu.get_barrier_semaphore(), len(ROW_PEERS) + 7)


def remote(src, dst, ss, rs, dev):
    return pltpu.make_async_remote_copy(
        src_ref=src, dst_ref=dst, send_sem=ss, recv_sem=rs, device_id=dev, device_id_type=MESH
    )


class Exchange:
    def __init__(self, me, src, dst, land, ss, rs, base):
        self.me, self.src, self.dst, self.land = me, src, dst, land
        self.ss, self.rs, self.base = ss, rs, base

    def _copy(self, d):
        return remote(
            self.src(d),
            self.dst(d),
            self.ss.at[self.base + d - 1],
            self.rs.at[self.base + d - 1],
            self.me.seq_dev(d),
        )

    def start(self):
        for d in range(1, 8):
            self._copy(d).start()

    def wait_recv(self):
        for d in range(1, 8):
            here = self.land(d)
            remote(
                here, here, self.ss.at[self.base + d - 1], self.rs.at[self.base + d - 1], self.me.seq_dev(d)
            ).wait_recv()

    def wait_send(self):
        for d in range(1, 8):
            self._copy(d).wait_send()


GATHER_SEMS = 17


class RowsGather:
    def __init__(self, me, buf, cut, ss, rs, base, core=True):
        self.me, self.buf, self.cut, self.core = me, buf, cut, core
        self.ss, self.rs, self.base = ss, rs, base
        self.sent = []

    def _part(self, rel, part):
        slot = self.me.slot(*rel)
        full = self.buf.shape[1]
        if part == 0:
            return self.buf.at[slot]
        if part == 1:
            return self.buf.at[slot, pl.ds(0, self.cut)]
        return self.buf.at[slot, pl.ds(self.cut, full - self.cut)]

    PLAN = {
        "y": (0, (0, 1, 0), (0, 0, 0), 0),
        "p0": (1, (1, 0, 0), (0, 0, 0), 0),
        "m0": (2, (3, 0, 0), (0, 0, 0), 0),
        "p1": (3, (1, 0, 0), (0, 1, 0), 0),
        "m1": (4, (3, 0, 0), (0, 1, 0), 0),
        "fp0": (5, (1, 0, 0), (3, 0, 0), 1),
        "fm0": (6, (3, 0, 0), (1, 0, 0), 2),
        "fp1": (7, (1, 0, 0), (3, 1, 0), 1),
        "fm1": (8, (3, 0, 0), (1, 1, 0), 2),
        "c00": (9, (0, 0, 1), (0, 0, 0), 0),
        "c01": (10, (0, 0, 1), (0, 1, 0), 0),
        "c10": (11, (0, 0, 1), (1, 0, 0), 0),
        "c11": (12, (0, 0, 1), (1, 1, 0), 0),
        "c20": (13, (0, 0, 1), (2, 0, 0), 0),
        "c21": (14, (0, 0, 1), (2, 1, 0), 0),
        "c30": (15, (0, 0, 1), (3, 0, 0), 0),
        "c31": (16, (0, 0, 1), (3, 1, 0), 0),
    }

    def _send(self, name):
        i, to, block, part = self.PLAN[name]
        ref = self._part(block, part)
        return remote(ref, ref, self.ss.at[self.base + i], self.rs.at[self.base + i], self.me.row_dev(*to))

    def send(self, *names):
        for name in names:
            if self.core or name[0] != "c":
                self._send(name).start()
                self.sent.append(name)

    def recv(self, *names):
        for name in names:
            i, to, block, part = self.PLAN[name]
            rel = ((block[0] - to[0]) % 4, (block[1] - to[1]) % 2, (block[2] - to[2]) % 2)
            ref = self._part(rel, part)
            remote(ref, ref, self.ss.at[self.base + i], self.rs.at[self.base + i], self.me.row_dev(*to)).wait_recv()

    def step0(self):
        self.send("p0", "m0", "y", "c00")

    def step1(self):
        self.recv("y")
        self.send("p1", "m1", "c01")

    def step2(self):
        self.recv("p0")
        self.send("fp0", "c30")
        self.recv("m0")
        self.send("fm0", "c10")

    def step3(self):
        self.recv("p1")
        self.send("fp1", "c31")
        self.recv("m1")
        self.send("fm1", "c11")

    def step4(self):
        self.recv("fp0", "fm0")
        self.send("c20")

    def step5(self):
        self.recv("fp1", "fm1")
        self.send("c21")

    def step6(self):
        self.recv("c00", "c01", "c10", "c11", "c20", "c21", "c30", "c31")

    def finish(self):
        for name in self.sent:
            self._send(name).wait_send()


class RowsScatter:
    def __init__(self, me, g, cr, zlo, zhi, zr, yr, ss, rs, base, first=0):
        self.me, self.g, self.cr, self.zlo, self.zhi, self.zr, self.yr = me, g, cr, zlo, zhi, zr, yr
        self.ss, self.rs, self.base = ss, rs, base
        cut, rows = zlo.shape[1], yr.shape[0]
        self.all, self.lo, self.hi = pl.ds(first, rows), pl.ds(first, cut), pl.ds(first + cut, rows - cut)
        self.open = []

    def _copy(self, i, src, dst, to):
        return remote(src, dst, self.ss.at[self.base + i], self.rs.at[self.base + i], self.me.row_dev(*to))

    def _start(self, i, src, dst, to):
        copy = self._copy(i, src, dst, to)
        copy.start()
        self.open.append(copy)

    def _landed(self, i, dst, to):
        self._copy(i, dst, dst, to).wait_recv()

    ORDER = ((2, 0), (2, 1), (1, 0), (1, 1), (3, 0), (3, 1), (0, 1), (0, 0))

    def start_core(self):
        for k, (dz, dy) in enumerate(self.ORDER):
            self._start(k, self.g.at[self.me.slot(dz, dy, 1), self.all], self.cr.at[k], (0, 0, 1))

    def _add(self, k):
        if self.cr is None:
            return
        dz, dy = self.ORDER[k]
        self._landed(k, self.cr.at[k], (0, 0, 1))
        slot = self.me.slot(dz, dy, 0)
        self.g[slot, self.all] = (self.g[slot, self.all].astype(F32) + self.cr[k].astype(F32)).astype(BF)

    def add_far(self):
        for dy in (0, 1):
            self._add(dy)
            slot = self.me.slot(2, dy, 0)
            self._start(8 + dy, self.g.at[slot, self.lo], self.zlo.at[dy], (1, 0, 0))
            self._start(10 + dy, self.g.at[slot, self.hi], self.zhi.at[dy], (3, 0, 0))

    def add_near(self):
        for k in (2, 3, 4, 5):
            self._add(k)

    def pass_near(self):
        for dy in (1, 0):
            self._landed(8 + dy, self.zlo.at[dy], (1, 0, 0))
            slot = self.me.slot(1, dy, 0)
            self.g[slot, self.lo] = (self.g[slot, self.lo].astype(F32) + self.zlo[dy].astype(F32)).astype(BF)
            self._start(12 + 2 * dy, self.g.at[slot, self.all], self.zr.at[0, dy], (1, 0, 0))
            self._landed(10 + dy, self.zhi.at[dy], (3, 0, 0))
            slot = self.me.slot(3, dy, 0)
            self.g[slot, self.hi] = (self.g[slot, self.hi].astype(F32) + self.zhi[dy].astype(F32)).astype(BF)
            self._start(13 + 2 * dy, self.g.at[slot, self.all], self.zr.at[1, dy], (3, 0, 0))

    def own_core(self):
        self._add(6)
        self._add(7)

    def cross(self):
        self._landed(14, self.zr.at[0, 1], (1, 0, 0))
        self._landed(15, self.zr.at[1, 1], (3, 0, 0))
        slot = self.me.slot(0, 1, 0)
        total = self.g[slot, self.all].astype(F32) + self.zr[0, 1].astype(F32) + self.zr[1, 1].astype(F32)
        self.g[slot, self.all] = total.astype(BF)
        self._start(16, self.g.at[slot, self.all], self.yr, (0, 1, 0))

    def last(self):
        self._landed(12, self.zr.at[0, 0], (1, 0, 0))
        self._landed(13, self.zr.at[1, 0], (3, 0, 0))
        self._landed(16, self.yr, (0, 1, 0))
        slot = self.me.slot(0, 0, 0)
        return (
            self.g[slot, self.all].astype(F32)
            + self.zr[0, 0].astype(F32)
            + self.zr[1, 0].astype(F32)
            + self.yr[...].astype(F32)
        )

    def finish(self):
        for copy in self.open:
            copy.wait_send()


SCATTER_SEMS = 17


def small_vec(refs):
    lane = lax.broadcasted_iota(jnp.int32, (1, 128), 1)
    out = jnp.zeros((1, 128), F32)
    for p, ref in enumerate(refs):
        for i in range(6):
            out = jnp.where(lane == p * 32 + i, ref[i], out)
    return out


def normalise(v):
    mean = jnp.mean(v, axis=-1, keepdims=True)
    centred = v - mean
    var = jnp.mean(centred * centred, axis=-1, keepdims=True)
    inverse = lax.rsqrt(var + EPS)
    return centred * inverse, inverse


SCALE = HEAD_DIM**-0.5
LOG2E = 1.4426950408889634
BASE = (0, 256, 768, 1536)


def lanes(ref, b, c, h, first, count):
    rows = pl.ds(pl.multiple_of(h * 32, 32), 32)
    if c is None:
        parts = [ref[b, first + i, rows, :] for i in range(count)]
    else:
        parts = [ref[b, first + i, c, rows, :] for i in range(count)]
    return parts[0] if count == 1 else jnp.concatenate(parts, axis=1)


def allowed(nk, length):
    key = lax.broadcasted_iota(jnp.int32, (nk, 256), 0)
    query = lax.broadcasted_iota(jnp.int32, (nk, 256), 1) + (nk - 256)
    return (key <= query) & (key < length)


def attend_one(heads_ref, length, p_ref, l_ref, os_ref, b, h, i):
    rows = pl.ds(pl.multiple_of(h * 32, 32), 32)
    kt = lanes(heads_ref, b, 1, h, 0, 8)
    vt = lanes(heads_ref, b, 2, h, 0, 8)
    for qb in range(4):
        nk = (qb + 1) * 256
        qt = lanes(heads_ref, b, 0, h, 2 * qb, 2)
        s = tn(kt[:, :nk], qt)
        s = jnp.where(allowed(nk, length), s, -1e30)
        top = jnp.max(s, axis=0, keepdims=True)
        p = jnp.exp2((s - top) * (SCALE * LOG2E))
        inverse = 1.0 / jnp.sum(p, axis=0, keepdims=True)
        low = p.astype(BF)
        p_ref[i, pl.ds(BASE[qb], nk), :] = low
        l_ref[i, pl.ds(qb, 1), :] = inverse
        o = (nn(vt[:, :nk], low) * inverse).astype(BF)
        os_ref[b, 2 * qb, rows, :] = o[:, :128]
        os_ref[b, 2 * qb + 1, rows, :] = o[:, 128:]


def attend_one_back(heads_ref, p_ref, l_ref, os_ref, do_ref, dq_ref, acc_ref, b, h, i):
    rows = pl.ds(pl.multiple_of(h * 32, 32), 32)
    kt = lanes(heads_ref, b, 1, h, 0, 8)
    vt = lanes(heads_ref, b, 2, h, 0, 8)
    for qb in range(4):
        nk = (qb + 1) * 256
        qt = lanes(heads_ref, b, 0, h, 2 * qb, 2)
        do = lanes(do_ref, b, None, h, 2 * qb, 2).astype(F32) * l_ref[i, pl.ds(qb, 1), :]
        o = lanes(os_ref, b, None, h, 2 * qb, 2).astype(F32)
        delta = jnp.sum(do * o, axis=0, keepdims=True)
        low = do.astype(BF)
        p = p_ref[i, pl.ds(BASE[qb], nk), :]
        ds = (p.astype(F32) * (tn(vt[:, :nk], low) - delta)).astype(BF)
        dv = nt(low, p)
        dk = nt(qt, ds)
        if nk > 256:
            acc_ref[0, :, : nk - 256] += dk[:, : nk - 256]
            acc_ref[1, :, : nk - 256] += dv[:, : nk - 256]
        acc_ref[0, :, nk - 256 : nk] = dk[:, nk - 256 :]
        acc_ref[1, :, nk - 256 : nk] = dv[:, nk - 256 :]
        dq = (nn(kt[:, :nk], ds) * SCALE).astype(BF)
        dq_ref[2 * qb, 0, rows, :] = dq[:, :128]
        dq_ref[2 * qb + 1, 0, rows, :] = dq[:, 128:]
    for j in range(8):
        dq_ref[j, 1, rows, :] = (acc_ref[0, :, j * 128 : (j + 1) * 128] * SCALE).astype(BF)
        dq_ref[j, 2, rows, :] = acc_ref[1, :, j * 128 : (j + 1) * 128].astype(BF)


def feed_forward(first, end, gu_ref, gw_ref, h2_ref, dy_ref, y_ref, dh_ref):
    def block(j, carry):
        up = pl.ds(pl.multiple_of(j * 48, 16), 48)
        deep = pl.ds(j * 4, 4)
        wu = gu_ref[:, up, :].reshape(768, 768)
        h2 = h2_ref[...]
        u = nn(h2, wu)
        phi = 0.5 + 0.5 * lax.erf(u * (1.0 / math.sqrt(2.0)))
        act = (u * phi).astype(BF)
        slope = phi + u * jnp.exp(-0.5 * u * u) * (1.0 / math.sqrt(2.0 * math.pi))
        wd = gw_ref[deep].reshape(768, 768)
        dy = dy_ref[...].reshape(256, 768)
        y_ref[...] += nn(act, wd)
        du = (nt(dy, wd) * slope).astype(BF)
        gw_ref[deep] = tn(act, dy).astype(BF).reshape(4, 192, 768)
        dh_ref[...] += nt(du, wu)
        gu_ref[:, up, :] = tn(h2, du).astype(BF).reshape(16, 48, 768)
        return carry

    lax.fori_loop(first, end, block, 0)


def norm_parts(grad, gain, scaled, inverse):
    weighted = grad * gain
    first = jnp.mean(weighted, axis=-1, keepdims=True)
    second = jnp.mean(weighted * scaled, axis=-1, keepdims=True)
    grad_in = inverse * (weighted - first - scaled * second)
    return grad_in, jnp.sum(grad * scaled, axis=0, keepdims=True), jnp.sum(grad, axis=0, keepdims=True)


HBM = pl.BlockSpec(memory_space=pl.ANY)


class Counter:
    def __init__(self):
        self.n = 0

    def take(self, k):
        first = self.n
        self.n += k
        return first


def plan():
    c = Counter()
    at = {}
    for name in ("xa", "xu", "xw", "sa", "su", "sw"):
        at[name] = c.take(7)
    for name in ("ga", "gu", "gw", "gx0", "gx1"):
        at[name] = c.take(GATHER_SEMS)
    for name in ("o", "do"):
        at[name] = c.take(14)
    for name in ("ra", "ru1", "ru2", "rw", "rx0", "rx1"):
        at[name] = c.take(SCATTER_SEMS)
    return at, c.n


def scatter_scratch(rows, cut, wide, core=True):
    made = [
        pltpu.VMEM((2, cut, wide), BF),
        pltpu.VMEM((2, rows - cut, wide), BF),
        pltpu.VMEM((2, 2, rows, wide), BF),
        pltpu.VMEM((rows, wide), BF),
    ]
    return ([pltpu.VMEM((8, rows, wide), BF)] if core else []) + made


CUT_A, CUT_U, CUT_W, CUT_X = 80, 128, 96, 64
U1, U2 = 96, 144
SCRATCH = dict(
    xl=pltpu.VMEM((2, 8, 128, 768), BF),
    h1=pltpu.VMEM((2, 8, 128, 768), BF),
    dy=pltpu.VMEM((2, 128, 768), BF),
    wq=pltpu.VMEM((6, 3, 768), F32),
    wo=pltpu.VMEM((6, 768), F32),
    wu=pltpu.VMEM((6, 3072), F32),
    wd=pltpu.VMEM((24, 768), F32),
    pa=pltpu.VMEM((ROWS_A, 256), BF),
    pu=pltpu.VMEM((ROWS_U, 256), BF),
    pw=pltpu.VMEM((ROWS_W, 256), BF),
    sm=pltpu.VMEM((256, 768), BF),
    se=pltpu.VMEM((4, 128, 768), BF),
    ge=pltpu.VMEM((768, 1024), BF),
    f=pltpu.VMEM((96, 768), F32),
    fl=pltpu.VMEM((32, 128), F32),
    ka=pltpu.VMEM((8, 32, 128), BF),
    k=pltpu.VMEM((2, 32, 768), BF),
    xa=pltpu.VMEM((8, 32, 128), BF),
    xu=pltpu.VMEM((8, 32, 768), BF),
    xw=pltpu.VMEM((8, 32, 768), BF),
    ga=pltpu.VMEM((16, ROWS_A, 128), BF),
    gu=pltpu.VMEM((16, ROWS_U, 768), BF),
    gw=pltpu.VMEM((16, ROWS_W, 768), BF),
    lnp=pltpu.VMEM((8, 768), F32),
    wt=pltpu.VMEM((288, 768), BF),
    dwt=pltpu.VMEM((3, 128, 768), F32),
    xhat=pltpu.VMEM((256, 768), F32),
    inv=pltpu.VMEM((256, 1), F32),
    heads=pltpu.VMEM((2, 8, 3, 96, 128), BF),
    p=pltpu.VMEM((6, 2560, 256), BF),
    l=pltpu.VMEM((6, 4, 256), F32),
    os=pltpu.VMEM((2, 8, 96, 128), BF),
    ot=pltpu.VMEM((2, 8, 96, 128), BF),
    h2=pltpu.VMEM((256, 768), BF),
    xh2=pltpu.VMEM((256, 768), F32),
    y=pltpu.VMEM((256, 768), F32),
    dh=pltpu.VMEM((256, 768), F32),
    dot=pltpu.VMEM((2, 8, 96, 128), BF),
    do=pltpu.VMEM((2, 8, 96, 128), BF),
    acc=pltpu.VMEM((2, 32, 1024), F32),
    dq=pltpu.VMEM((8, 3, 96, 128), BF),
    lng=pltpu.VMEM((8, 768), F32),
    xsa=pltpu.VMEM((8, 32, 128), BF),
    xs=pltpu.VMEM((2, 8, 32, 768), BF),
)
SMALL = dict(
    len=pltpu.SMEM((2,), jnp.int32),
    g1=pltpu.SMEM((6,), F32),
    b1=pltpu.SMEM((6,), F32),
    g2=pltpu.SMEM((6,), F32),
    b2=pltpu.SMEM((6,), F32),
)
INPUTS = ("x", "wq", "g1", "b1", "g2", "b2", "ge", "wu", "wo", "wd", "pa", "pu", "pw", "sm", "se", "dy", "len")


def feature_major(ref, b):
    return ref[b].reshape(768, 128)


def layer_kernel(*refs):
    inputs = dict(zip(INPUTS, refs))
    refs = refs[len(INPUTS) :]
    out_ref, ig_ref, sum_ref = refs[:3]
    names = [*SCRATCH, *SMALL]
    v = dict(zip(names, refs[3 : 3 + len(names)]))
    rest = refs[3 + len(names) :]
    scr_a, scr_u1, scr_u2, scr_w = rest[:5], rest[5:10], rest[10:15], rest[15:20]
    scr_x = (rest[20:24], rest[24:28])
    ss, rs, ls = rest[28:]
    at, _ = plan()
    me = Place()
    seq = me.along_seq()
    barrier_signal(me)
    xl = v["xl"]
    loads = {}
    for b in range(2):
        loads[b] = pltpu.make_async_copy(inputs["x"].at[b], xl.at[b, me.s], ls.at[21 + b])
        loads[b].start()
    for i, name in enumerate(INPUTS):
        if name != "x":
            loads[name] = pltpu.make_async_copy(inputs[name], v[name], ls.at[i])
            loads[name].start()

    def loaded(*which):
        for name in which:
            loads[name].wait()

    def seq_gather(src, dst, key):
        made = Exchange(me, lambda d: src, lambda d: dst.at[me.s], lambda d: dst.at[me.seq_at(8 - d)], ss, rs, at[key])
        made.start()
        dst[me.s] = src[...]
        return made

    def seq_scatter(src, dst, key):
        made = Exchange(
            me, lambda d: src.at[me.seq_at(d)], lambda d: dst.at[me.s], lambda d: dst.at[me.seq_at(8 - d)], ss, rs, at[key]
        )
        made.start()
        dst[me.s] = src[me.s]
        return made

    def by_row(src, dst, key):
        return [
            Exchange(
                me,
                lambda d, b=b: src.at[b, me.seq_at(d)],
                lambda d, b=b: dst.at[b, me.s],
                lambda d, b=b: dst.at[b, me.seq_at(8 - d)],
                ss,
                rs,
                at[key] + 7 * b,
            )
            for b in range(2)
        ]

    f, fl = v["f"], v["fl"]
    f[...] = jnp.zeros_like(f)
    fl[...] = jnp.zeros_like(fl)
    ga, gu, gw = v["ga"], v["gu"], v["gw"]
    ag_x = [RowsGather(seq, xl.at[b], CUT_X, ss, rs, at[f"gx{b}"], core=False) for b in range(2)]
    ag_a = RowsGather(me, ga, CUT_A, ss, rs, at["ga"])
    ag_u = RowsGather(me, gu, CUT_U, ss, rs, at["gu"])
    ag_w = RowsGather(me, gw, CUT_W, ss, rs, at["gw"])
    loaded(0)
    barrier_wait()
    ag_x[0].step0()
    loaded("wq", "g1", "b1", "g2", "b2", "ge")
    for c in range(3):
        for i in range(6):
            f[pl.ds(c * 6 + i, 1), :] = v["wq"][i, pl.ds(c, 1), :]
    fl[pl.ds(18, 1), :] = small_vec([v[name] for name in ("g1", "b1", "g2", "b2")])
    wide = nn(f[pl.ds(0, 32), :].astype(BF), v["ge"][...])
    for k in range(8):
        v["ka"][k] = (wide[:, k * 128 : (k + 1) * 128] + fl[...]).astype(BF)
    x_a = seq_scatter(v["ka"], v["xa"], "xa")
    loaded("wu", "wo", "wd")
    for j in range(4):
        f[pl.ds(32 + j * 6, 6), :] = v["wu"][:, pl.ds(j * 768, 768)]
    f[pl.ds(56, 6), :] = v["wo"][...]
    f[pl.ds(64, 24), :] = v["wd"][...]
    v["k"][0] = f[pl.ds(32, 32), :].astype(BF)
    v["k"][1] = f[pl.ds(64, 32), :].astype(BF)
    x_u = seq_gather(v["k"].at[0], v["xu"], "xu")
    x_w = seq_gather(v["k"].at[1], v["xw"], "xw")
    loaded(1, "pa", "pu", "pw", "sm", "se", "dy", "len")
    ag_x[0].step1()
    x_a.wait_recv()
    ga[me.r] = nn(v["pa"][...], v["xa"][...].reshape(256, 128)).astype(BF)
    ag_a.step0()
    ag_x[0].step2()
    for b in range(2):
        xhat, inverse = normalise(xl[b, me.s].astype(F32))
        v["xhat"][pl.ds(b * 128, 128), :] = xhat
        v["inv"][pl.ds(b * 128, 128), :] = inverse
    x_u.wait_recv()
    gu[me.r] = nn(v["pu"][...], v["xu"][...].reshape(256, 768)).astype(BF)
    ag_a.step1()
    ag_u.step0()
    ag_a.step2()
    x_w.wait_recv()
    gw[me.r] = nn(v["pw"][...], v["xw"][...].reshape(256, 768)).astype(BF)
    ag_a.step3()
    ag_w.step0()
    ag_x[1].step0()
    ag_x[0].step3()
    ag_a.step4()
    ag_a.step5()
    ag_u.step1()
    ag_a.step6()

    lnp = v["lnp"]
    ln = ga[:, pl.ds(144, 16), :].reshape(256, 128)
    for p in range(4):
        spread = nn(ln, v["se"][p])
        lnp[pl.ds(p, 1), :] = jnp.sum(spread * v["sm"][...].astype(F32), axis=0, keepdims=True)
    for c in range(3):
        w = ga[:, pl.ds(c * 48, 48), :].reshape(768, 128)
        v["wt"][pl.ds(c * 96, 96), :] = w.T[:96]

    def prepare(b, slot):
        xhat, _ = normalise(xl[b, slot].astype(F32))
        h = (xhat * lnp[pl.ds(0, 1), :] + lnp[pl.ds(1, 1), :]).astype(BF)
        v["h1"][b, slot] = h
        v["heads"][b, slot] = nt(v["wt"][...], h).astype(BF).reshape(3, 96, 128)

    def prepare_pair(b, dx, dy, step_x, step_y):
        def one(i, carry):
            prepare(b, seq.slot(dx + i * step_x, dy + i * step_y, 0))
            return carry

        lax.fori_loop(0, 2, one, 0)

    x_o = by_row(v["os"], v["ot"], "o")

    def forward(b):
        def one(h, carry):
            attend_one(v["heads"], v["len"][b], v["p"], v["l"], v["os"], b, h, b * 3 + h)
            return carry

        lax.fori_loop(0, 3, one, 0)
        x_o[b].start()
        v["ot"][b, me.s] = v["os"][b, me.s]

    prepare_pair(0, 0, 0, 0, 1)
    prepare_pair(0, 1, 0, 2, 0)
    prepare_pair(0, 1, 1, 2, 0)
    ag_w.step1()
    ag_x[1].step1()
    ag_x[0].step4()
    ag_x[0].step5()
    prepare_pair(0, 2, 0, 0, 1)
    ag_x[1].step2()
    ag_u.step2()
    forward(0)
    ag_w.step2()
    ag_x[1].step3()
    prepare_pair(1, 0, 0, 0, 1)
    prepare_pair(1, 1, 0, 2, 0)
    prepare_pair(1, 1, 1, 2, 0)
    ag_u.step3()
    ag_x[1].step4()
    ag_x[1].step5()
    prepare_pair(1, 2, 0, 0, 1)
    ag_w.step3()
    forward(1)
    ag_u.step4()
    ag_u.step5()
    for b in range(2):
        x_o[b].wait_recv()
    ag_u.step6()

    ot = jnp.concatenate([feature_major(v["ot"], b) for b in range(2)], axis=1)
    wo = gu[:, pl.ds(192, 48), :].reshape(768, 768)
    x1 = jnp.concatenate([xl[b, me.s] for b in range(2)], axis=0).astype(F32) + tn(ot, wo)
    xhat2, inverse2 = normalise(x1)
    v["xh2"][...] = xhat2
    v["h2"][...] = (xhat2 * lnp[pl.ds(2, 1), :] + lnp[pl.ds(3, 1), :]).astype(BF)
    v["y"][...] = x1
    v["dh"][...] = jnp.zeros_like(v["dh"])
    ag_w.step4()
    ag_w.step5()
    ag_w.step6()
    ag_u.finish()
    ag_w.finish()
    rs_u1 = RowsScatter(me, gu, *scr_u1, ss, rs, at["ru1"])
    rs_u2 = RowsScatter(me, gu, *scr_u2, ss, rs, at["ru2"], U1)
    rs_w = RowsScatter(me, gw, *scr_w, ss, rs, at["rw"])
    rs_a = RowsScatter(me, ga, *scr_a, ss, rs, at["ra"])
    feed_forward(0, 2, gu, gw, v["h2"], v["dy"], v["y"], v["dh"])
    rs_u1.start_core()
    feed_forward(2, 4, gu, gw, v["h2"], v["dy"], v["y"], v["dh"])
    rs_w.start_core()
    rs_u1.add_far()
    rs_u1.add_near()
    grad_in, gg2, gb2 = norm_parts(v["dh"][...], lnp[pl.ds(2, 1), :], v["xh2"][...], inverse2)
    v["lng"][pl.ds(2, 1), :] = gg2
    v["lng"][pl.ds(3, 1), :] = gb2
    dx = v["dy"][...].reshape(256, 768).astype(F32) + grad_in
    v["xh2"][...] = dx
    low = dx.astype(BF)
    d = nt(wo, low).astype(BF)
    for k in range(8):
        for b in range(2):
            v["dot"][b, k] = d[k * 96 : (k + 1) * 96, b * 128 : (b + 1) * 128]
    x_do = by_row(v["dot"], v["do"], "do")
    for b in range(2):
        x_do[b].start()
        v["do"][b, me.s] = v["dot"][b, me.s]
    rs_w.add_far()
    rs_u1.pass_near()
    gu[:, pl.ds(192, 48), :] = nn(ot, low).astype(BF).reshape(16, 48, 768)
    rs_u2.start_core()
    rs_w.add_near()
    v["h2"][...] = v["y"][...].astype(BF)
    stores = [pltpu.make_async_copy(v["h2"].at[pl.ds(b * 128, 128)], out_ref.at[b], ls.at[17 + b]) for b in range(2)]
    for b in range(2):
        stores[b].start()
    rs_u2.add_far()
    rs_u2.add_near()
    rs_w.pass_near()

    v["dwt"][...] = jnp.zeros_like(v["dwt"])
    v["lng"][pl.ds(0, 2), :] = jnp.zeros((2, 768), F32)
    dq_ref = v["dq"]

    def one_back(b, slot):
        grad = tn(dq_ref[slot].reshape(288, 128), v["wt"][...])
        v["lng"][pl.ds(0, 1), :] += jnp.sum(grad * v["h1"][b, slot].astype(F32), axis=0, keepdims=True)
        v["lng"][pl.ds(1, 1), :] += jnp.sum(grad, axis=0, keepdims=True)
        xl[b, slot] = grad.astype(BF)

    rs_x = [RowsScatter(seq, xl.at[b], None, *scr_x[b], ss, rs, at[f"rx{b}"]) for b in range(2)]

    def backward(b):
        x_do[b].wait_recv()
        ag_x[b].finish()

        def one(h, carry):
            attend_one_back(v["heads"], v["p"], v["l"], v["os"], v["do"], dq_ref, v["acc"], b, h, b * 3 + h)
            return carry

        lax.fori_loop(0, 3, one, 0)

        def far(i, carry):
            one_back(b, seq.slot(2, i, 0))
            return carry

        def near(i, carry):
            one_back(b, seq.slot((1 + 2 * (i // 2)) % 5, i, 0))
            return carry

        lax.fori_loop(0, 2, far, 0)
        rs_x[b].add_far()
        lax.fori_loop(0, 6, near, 0)
        grad = jnp.concatenate([dq_ref[i].reshape(288, 128) for i in range(8)], axis=1)
        dw = nn(grad, v["h1"][b].reshape(1024, 768))
        for c in range(3):
            v["dwt"][c, pl.ds(0, 96), :] += dw[c * 96 : (c + 1) * 96]

    backward(0)
    rs_u1.own_core()
    rs_u1.cross()
    rs_u2.pass_near()
    rs_x[0].pass_near()
    backward(1)

    def norm1_back(b):
        rows = pl.ds(b * 128, 128)
        grad = rs_x[b].last()
        grad_in, _, _ = norm_parts(grad, lnp[pl.ds(0, 1), :], v["xhat"][rows, :], v["inv"][rows, :])
        v["xhat"][rows, :] = v["xh2"][rows, :] + grad_in
        stores.append(pltpu.make_async_copy(v["xhat"].at[rows], ig_ref.at[b], ls.at[19 + b]))
        stores[2 + b].start()

    ag_a.finish()
    for c in range(3):
        ga[:, pl.ds(c * 48, 48), :] = v["dwt"][c].T.astype(BF).reshape(16, 48, 128)
    lng = v["lng"]
    lng[pl.ds(0, 1), :] = (lng[pl.ds(0, 1), :] - lnp[pl.ds(1, 1), :] * lng[pl.ds(1, 1), :]) / lnp[pl.ds(0, 1), :]
    parts = jnp.zeros((256, 128), F32)
    for p in range(4):
        parts += nt((v["sm"][...].astype(F32) * lng[pl.ds(p, 1), :]).astype(BF), v["se"][p])
    ga[:, pl.ds(144, 16), :] = parts.astype(BF).reshape(16, 16, 128)
    rs_a.start_core()
    def scatter_rows(ref, perm, rows):
        ref[...] = tn(perm[...], rows.astype(BF)).astype(BF).reshape(ref.shape)

    rs_w.own_core()
    rs_w.cross()
    rs_a.add_far()
    rs_a.add_near()
    rs_x[0].cross()
    rs_x[1].pass_near()
    rs_a.pass_near()
    rs_a.own_core()
    scatter_rows(v["xw"], v["pw"], rs_w.last())
    s_w = seq_scatter(v["xw"], v["xs"].at[1], "sw")
    rs_u2.own_core()
    rs_u2.cross()
    rs_a.cross()
    norm1_back(0)
    rs_x[1].cross()
    total = jnp.concatenate([rs_u1.last(), rs_u2.last()], axis=0)
    scatter_rows(v["xu"], v["pu"], total)
    s_u = seq_scatter(v["xu"], v["xs"].at[0], "su")
    scatter_rows(v["xa"], v["pa"], rs_a.last())
    s_a = seq_scatter(v["xa"], v["xsa"], "sa")
    norm1_back(1)
    s_w.wait_recv()
    f[pl.ds(64, 32), :] = jnp.sum(v["xs"][1].astype(F32), axis=0)
    s_a.wait_recv()
    packets = jnp.concatenate([v["xsa"][k] for k in range(8)], axis=1)
    f[pl.ds(0, 32), :] = nt(packets, v["ge"][...])
    fl[...] = jnp.sum(v["xsa"][...].astype(F32), axis=0)
    f[pl.ds(24, 1), pl.ds(0, 128)] = fl[pl.ds(18, 1), :]
    s_u.wait_recv()
    f[pl.ds(32, 32), :] = jnp.sum(v["xs"][0].astype(F32), axis=0)
    stores.append(pltpu.make_async_copy(f, sum_ref, ls.at[0]))
    stores[4].start()
    for each in (x_a, x_u, x_w, *x_o, *x_do, s_a, s_u, s_w):
        each.wait_send()
    for each in (rs_a, rs_u1, rs_u2, rs_w, *rs_x):
        each.finish()
    for store in stores:
        store.wait()


def final_kernel(out_in, ig_in, f_in, out_ref, ig_ref, dwq_ref, dwo_ref, dwu_ref, dwd_ref, ln_ref, out_v, ig_v, f_ref, sem):
    loads = [
        pltpu.make_async_copy(src, dst, sem.at[i])
        for i, (src, dst) in enumerate(((f_in, f_ref), (ig_in, ig_v), (out_in, out_v)))
    ]
    for load in loads:
        load.start()
    a = pltpu.make_async_copy(out_v, out_ref, sem.at[3])
    b = pltpu.make_async_copy(ig_v, ig_ref, sem.at[4])
    loads[1].wait()
    b.start()
    loads[2].wait()
    a.start()
    loads[0].wait()
    for c in range(3):
        for i in range(6):
            dwq_ref[i, pl.ds(c, 1), :] = f_ref[pl.ds(c * 6 + i, 1), :]
    ln_ref[...] = f_ref[pl.ds(24, 8), :]
    for j in range(4):
        dwu_ref[:, pl.ds(j * 768, 768)] = f_ref[pl.ds(32 + j * 6, 6), :]
    dwo_ref[...] = f_ref[pl.ds(56, 6), :]
    dwd_ref[...] = f_ref[pl.ds(64, 24), :]
    a.wait()
    b.wait()


def on_device(inputs, lengths, qkv_weight, out_weight, up_weight, down_weight, ln1_gain, ln1_bias, ln2_gain, ln2_bias, cotangent):
    sds = jax.ShapeDtypeStruct
    n = plan()[1]
    given = dict(
        x=inputs, dy=cotangent, wq=qkv_weight, wo=out_weight, wu=up_weight, wd=down_weight,
        g1=ln1_gain, b1=ln1_bias, g2=ln2_gain, b2=ln2_bias, len=lengths,
        pa=const(perm_a()), pu=const(perm_u()), pw=const(perm_w()), sm=const(spread_m()), se=const(spread_e()), ge=const(groups_e()),
    )
    out, ig, sums = pl.pallas_call(
        layer_kernel,
        out_shape=(sds((2, 128, 768), BF), sds((2, 128, 768), F32), sds((96, 768), F32)),
        in_specs=[HBM] * len(INPUTS),
        out_specs=[HBM] * 3,
        scratch_shapes=[
            *SCRATCH.values(),
            *SMALL.values(),
            *scatter_scratch(ROWS_A, CUT_A, 128),
            *scatter_scratch(U1, 48, 768),
            *scatter_scratch(U2, 80, 768),
            *scatter_scratch(ROWS_W, CUT_W, 768),
            *scatter_scratch(128, CUT_X, 768, core=False),
            *scatter_scratch(128, CUT_X, 768, core=False),
            pltpu.SemaphoreType.DMA((n,)),
            pltpu.SemaphoreType.DMA((n,)),
            pltpu.SemaphoreType.DMA((23,)),
        ],
        compiler_params=pltpu.CompilerParams(collective_id=0, has_side_effects=True, vmem_limit_bytes=63_000_000),
        name="layer",
    )(*[given[name] for name in INPUTS])
    res = pl.pallas_call(
        final_kernel,
        out_shape=(
            sds((2, 128, 768), BF), sds((2, 128, 768), F32), sds((6, 3, 768), F32), sds((6, 768), F32),
            sds((6, 3072), F32), sds((24, 768), F32), sds((8, 768), F32),
        ),
        in_specs=[HBM] * 3,
        out_specs=[HBM, HBM] + [VM] * 5,
        scratch_shapes=[
            pltpu.VMEM((2, 128, 768), BF),
            pltpu.VMEM((2, 128, 768), F32),
            pltpu.VMEM((96, 768), F32),
            pltpu.SemaphoreType.DMA((5,)),
        ],
        name="final",
    )(out, ig, sums)
    return (*res[:6], *[res[6][0, p * 32 : p * 32 + 6] for p in range(4)])


def solution(mesh):
    both = ("rows", "seq")
    return jax.shard_map(
        on_device,
        mesh=mesh,
        in_specs=(P("rows", "seq", None), P("rows"), P(both, None, None), P(both, None), P(both, None), P(both, None),
                  P(both), P(both), P(both), P(both), P("rows", "seq", None)),
        out_specs=(P("rows", "seq", None), P("rows", "seq", None), P(both, None, None), P(both, None), P(both, None),
                   P(both, None), P(both), P(both), P(both), P(both)),
        check_vma=False,
    )
```

time: 178 us -> 159 us (0.89)
  Pallas kernels: 176 us -> 156 us
    pallas_call x1, Pallas kernels: 173 us -> 153 us  [on_device(): pl.pallas_call(layer_kernel, out_shape=(sds((2, 128, 768), BF), sds((2, 1...]
where the time goes in v1:
time: 159 us; the launch traced here: 158 us
  Pallas kernels  156 us (98%)
    pallas_call x1, Pallas kernels, on_device(): pl.pallas_call(layer_kernel, out_shape=(sds((2, 128, 768), BF), sds((2, 1...  153 us

profile of v1, /device:TPU:0, one launch (start us, length us, event | category | flops | bytes accessed | tf_op | source)
XLA Modules:
  0.0 157.9 jit_solution(12302521607001317510)
XLA Ops:
  0.6 152.8 %layer.1 = (bf16[2,128,768]{2,1,0:T(8,128)(2,1)}, f32[2,128,768]{2,1,0:T(8,128)}, f32[96,768]{1,0:T(8,128)}) custom-call(bf16[2,128,768]{2,1,0:T(8,128)(2,1)} %refs_0_.1, f32[6,3,768]{2,1,0:T(4,128)} %refs_1_.1, f32[6]{0:T(128)} %refs_2_.1, f32[6]{0:T(128)} %refs_3_.1, f32[6]{0:T(128)} %refs_4_.1, f32[6]{0:T(128)} %refs_5_.1, ...), custom_call_target="tpu_custom_call" | custom-call | tf_op jit(solution)/shard_map/layer/pallas_call | solution.py:933
  153.5 3.0 %final.1 = (bf16[2,128,768]{2,1,0:T(8,128)(2,1)}, f32[2,128,768]{2,1,0:T(8,128)}, f32[6,3,768]{2,1,0:T(4,128)}, f32[6,768]{1,0:T(8,128)}, f32[6,3072]{1,0:T(8,12...) custom-call(bf16[2,128,768]{2,1,0:T(8,128)(2,1)} %get-tuple-element.20.out_in, f32[2,128,768]{2,1,0:T(8,128)} %get-tuple-element.21.ig_in, ...), custom_call_target="tpu_custom_call" | custom-call | tf_op jit(solution)/shard_map/final/pallas_call | solution.py:954
  156.5 1.4 slice_bitcast_fusion

commit v2 on v1

--- a/solution.py
+++ b/solution.py
@@ -125,7 +125,8 @@
         return {"seq": self.slot(dx, dy, dc)}
 
 
-ROW_PEERS = ((0, 0, 1), (0, 1, 0), (1, 0, 0), (3, 0, 0))
+NEAR = ((1, 0), (3, 0), (0, 1), (1, 1), (3, 1), (2, 0), (2, 1))
+ROW_PEERS = ((0, 0, 1), *[(dz, dy, 0) for dz, dy in NEAR])
 
 
 def barrier_signal(me):
@@ -352,6 +353,81 @@
 
 
 SCATTER_SEMS = 17
+
+
+class DirectGather:
+    SEMS = 15
+
+    def __init__(self, me, buf, ss, rs, base):
+        self.me, self.buf, self.ss, self.rs, self.base = me, buf, ss, rs, base
+        self.open = []
+
+    def _copy(self, i, rel, to):
+        block = self.buf.at[self.me.slot(*rel)]
+        return remote(block, block, self.ss.at[self.base + i], self.rs.at[self.base + i], self.me.row_dev(*to))
+
+    def _start(self, i, rel, to):
+        copy = self._copy(i, rel, to)
+        copy.start()
+        self.open.append(copy)
+
+    def start(self):
+        for k, (dz, dy) in enumerate(NEAR):
+            self._start(k, (0, 0, 0), (dz, dy, 0))
+        self._start(7, (0, 0, 0), (0, 0, 1))
+
+    def share(self):
+        for k, (dz, dy) in enumerate(NEAR):
+            self._copy(k, (4 - dz, dy, 0), (dz, dy, 0)).wait_recv()
+            self._start(8 + k, (4 - dz, dy, 0), (0, 0, 1))
+
+    def wait(self):
+        self._copy(7, (0, 0, 1), (0, 0, 1)).wait_recv()
+        for k, (dz, dy) in enumerate(NEAR):
+            self._copy(8 + k, (4 - dz, dy, 1), (0, 0, 1)).wait_recv()
+
+    def finish(self):
+        for copy in self.open:
+            copy.wait_send()
+
+
+class DirectScatter:
+    SEMS = 15
+
+    def __init__(self, me, g, cr, dr, ss, rs, base):
+        self.me, self.g, self.cr, self.dr, self.ss, self.rs, self.base = me, g, cr, dr, ss, rs, base
+        self.open = []
+
+    def _copy(self, i, src, dst, to):
+        return remote(src, dst, self.ss.at[self.base + i], self.rs.at[self.base + i], self.me.row_dev(*to))
+
+    def _start(self, i, src, dst, to):
+        copy = self._copy(i, src, dst, to)
+        copy.start()
+        self.open.append(copy)
+
+    def start_core(self):
+        for k, (dz, dy) in enumerate((*NEAR, (0, 0))):
+            self._start(k, self.g.at[self.me.slot(dz, dy, 1)], self.cr.at[k], (0, 0, 1))
+
+    def send(self):
+        for k, (dz, dy) in enumerate((*NEAR, (0, 0))):
+            self._copy(k, self.cr.at[k], self.cr.at[k], (0, 0, 1)).wait_recv()
+            slot = self.me.slot(dz, dy, 0)
+            self.g[slot] = (self.g[slot].astype(F32) + self.cr[k].astype(F32)).astype(BF)
+            if k < 7:
+                self._start(8 + k, self.g.at[slot], self.dr.at[k], (dz, dy, 0))
+
+    def last(self):
+        total = self.g[self.me.slot(0, 0, 0)].astype(F32)
+        for k, (dz, dy) in enumerate(NEAR):
+            self._copy(8 + k, self.dr.at[k], self.dr.at[k], (dz, dy, 0)).wait_recv()
+            total += self.dr[k].astype(F32)
+        return total
+
+    def finish(self):
+        for copy in self.open:
+            copy.wait_send()
 
 
 def small_vec(refs):
@@ -506,7 +582,7 @@
     return ([pltpu.VMEM((8, rows, wide), BF)] if core else []) + made
 
 
-CUT_A, CUT_U, CUT_W, CUT_X = 80, 128, 96, 64
+CUT_U, CUT_W, CUT_X = 128, 96, 64
 U1, U2 = 96, 144
 SCRATCH = dict(
     xl=pltpu.VMEM((2, 8, 128, 768), BF),
@@ -575,9 +651,9 @@
     names = [*SCRATCH, *SMALL]
     v = dict(zip(names, refs[3 : 3 + len(names)]))
     rest = refs[3 + len(names) :]
-    scr_a, scr_u1, scr_u2, scr_w = rest[:5], rest[5:10], rest[10:15], rest[15:20]
-    scr_x = (rest[20:24], rest[24:28])
-    ss, rs, ls = rest[28:]
+    scr_a, scr_u1, scr_u2, scr_w = rest[:2], rest[2:7], rest[7:12], rest[12:17]
+    scr_x = (rest[17:21], rest[21:25])
+    ss, rs, ls = rest[25:]
     at, _ = plan()
     me = Place()
     seq = me.along_seq()
@@ -629,12 +705,9 @@
     fl[...] = jnp.zeros_like(fl)
     ga, gu, gw = v["ga"], v["gu"], v["gw"]
     ag_x = [RowsGather(seq, xl.at[b], CUT_X, ss, rs, at[f"gx{b}"], core=False) for b in range(2)]
-    ag_a = RowsGather(me, ga, CUT_A, ss, rs, at["ga"])
+    ag_a = DirectGather(me, ga, ss, rs, at["ga"])
     ag_u = RowsGather(me, gu, CUT_U, ss, rs, at["gu"])
     ag_w = RowsGather(me, gw, CUT_W, ss, rs, at["gw"])
-    loaded(0)
-    barrier_wait()
-    ag_x[0].step0()
     loaded("wq", "g1", "b1", "g2", "b2", "ge")
     for c in range(3):
         for i in range(6):
@@ -643,7 +716,6 @@
     wide = nn(f[pl.ds(0, 32), :].astype(BF), v["ge"][...])
     for k in range(8):
         v["ka"][k] = (wide[:, k * 128 : (k + 1) * 128] + fl[...]).astype(BF)
-    x_a = seq_scatter(v["ka"], v["xa"], "xa")
     loaded("wu", "wo", "wd")
     for j in range(4):
         f[pl.ds(32 + j * 6, 6), :] = v["wu"][:, pl.ds(j * 768, 768)]
@@ -651,33 +723,31 @@
     f[pl.ds(64, 24), :] = v["wd"][...]
     v["k"][0] = f[pl.ds(32, 32), :].astype(BF)
     v["k"][1] = f[pl.ds(64, 32), :].astype(BF)
+    loaded(0, 1, "pa", "pu", "pw", "sm", "se", "dy", "len")
+    barrier_wait()
+    x_a = seq_scatter(v["ka"], v["xa"], "xa")
     x_u = seq_gather(v["k"].at[0], v["xu"], "xu")
     x_w = seq_gather(v["k"].at[1], v["xw"], "xw")
-    loaded(1, "pa", "pu", "pw", "sm", "se", "dy", "len")
-    ag_x[0].step1()
+    ag_x[0].step0()
     x_a.wait_recv()
     ga[me.r] = nn(v["pa"][...], v["xa"][...].reshape(256, 128)).astype(BF)
-    ag_a.step0()
+    ag_a.start()
+    x_u.wait_recv()
+    gu[me.r] = nn(v["pu"][...], v["xu"][...].reshape(256, 768)).astype(BF)
+    ag_u.step0()
+    ag_a.share()
+    x_w.wait_recv()
+    gw[me.r] = nn(v["pw"][...], v["xw"][...].reshape(256, 768)).astype(BF)
+    ag_w.step0()
+    ag_x[0].step1()
     ag_x[0].step2()
+    ag_x[1].step0()
     for b in range(2):
         xhat, inverse = normalise(xl[b, me.s].astype(F32))
         v["xhat"][pl.ds(b * 128, 128), :] = xhat
         v["inv"][pl.ds(b * 128, 128), :] = inverse
-    x_u.wait_recv()
-    gu[me.r] = nn(v["pu"][...], v["xu"][...].reshape(256, 768)).astype(BF)
-    ag_a.step1()
-    ag_u.step0()
-    ag_a.step2()
-    x_w.wait_recv()
-    gw[me.r] = nn(v["pw"][...], v["xw"][...].reshape(256, 768)).astype(BF)
-    ag_a.step3()
-    ag_w.step0()
-    ag_x[1].step0()
-    ag_x[0].step3()
-    ag_a.step4()
-    ag_a.step5()
+    ag_a.wait()
     ag_u.step1()
-    ag_a.step6()
 
     lnp = v["lnp"]
     ln = ga[:, pl.ds(144, 16), :].reshape(256, 128)
@@ -713,6 +783,7 @@
         v["ot"][b, me.s] = v["os"][b, me.s]
 
     prepare_pair(0, 0, 0, 0, 1)
+    ag_x[0].step3()
     prepare_pair(0, 1, 0, 2, 0)
     prepare_pair(0, 1, 1, 2, 0)
     ag_w.step1()
@@ -756,7 +827,7 @@
     rs_u1 = RowsScatter(me, gu, *scr_u1, ss, rs, at["ru1"])
     rs_u2 = RowsScatter(me, gu, *scr_u2, ss, rs, at["ru2"], U1)
     rs_w = RowsScatter(me, gw, *scr_w, ss, rs, at["rw"])
-    rs_a = RowsScatter(me, ga, *scr_a, ss, rs, at["ra"])
+    rs_a = DirectScatter(me, ga, *scr_a, ss, rs, at["ra"])
     feed_forward(0, 2, gu, gw, v["h2"], v["dy"], v["y"], v["dh"])
     rs_u1.start_core()
     feed_forward(2, 4, gu, gw, v["h2"], v["dy"], v["y"], v["dh"])
@@ -788,7 +859,6 @@
         stores[b].start()
     rs_u2.add_far()
     rs_u2.add_near()
-    rs_w.pass_near()
 
     v["dwt"][...] = jnp.zeros_like(v["dwt"])
     v["lng"][pl.ds(0, 2), :] = jnp.zeros((2, 768), F32)
@@ -802,7 +872,7 @@
 
     rs_x = [RowsScatter(seq, xl.at[b], None, *scr_x[b], ss, rs, at[f"rx{b}"]) for b in range(2)]
 
-    def backward(b):
+    def backward(b, between):
         x_do[b].wait_recv()
         ag_x[b].finish()
 
@@ -811,6 +881,7 @@
             return carry
 
         lax.fori_loop(0, 3, one, 0)
+        between()
 
         def far(i, carry):
             one_back(b, seq.slot(2, i, 0))
@@ -828,12 +899,15 @@
         for c in range(3):
             v["dwt"][c, pl.ds(0, 96), :] += dw[c * 96 : (c + 1) * 96]
 
-    backward(0)
+    def between():
+        rs_u2.pass_near()
+        rs_x[0].pass_near()
+        rs_w.own_core()
+
+    backward(0, rs_w.pass_near)
     rs_u1.own_core()
     rs_u1.cross()
-    rs_u2.pass_near()
-    rs_x[0].pass_near()
-    backward(1)
+    backward(1, between)
 
     def norm1_back(b):
         rows = pl.ds(b * 128, 128)
@@ -856,26 +930,21 @@
     def scatter_rows(ref, perm, rows):
         ref[...] = tn(perm[...], rows.astype(BF)).astype(BF).reshape(ref.shape)
 
-    rs_w.own_core()
+    rs_a.send()
     rs_w.cross()
-    rs_a.add_far()
-    rs_a.add_near()
+    rs_x[1].pass_near()
+    rs_u2.own_core()
     rs_x[0].cross()
-    rs_x[1].pass_near()
-    rs_a.pass_near()
-    rs_a.own_core()
+    rs_u2.cross()
     scatter_rows(v["xw"], v["pw"], rs_w.last())
     s_w = seq_scatter(v["xw"], v["xs"].at[1], "sw")
-    rs_u2.own_core()
-    rs_u2.cross()
-    rs_a.cross()
+    rs_x[1].cross()
+    scatter_rows(v["xa"], v["pa"], rs_a.last())
+    s_a = seq_scatter(v["xa"], v["xsa"], "sa")
     norm1_back(0)
-    rs_x[1].cross()
     total = jnp.concatenate([rs_u1.last(), rs_u2.last()], axis=0)
     scatter_rows(v["xu"], v["pu"], total)
     s_u = seq_scatter(v["xu"], v["xs"].at[0], "su")
-    scatter_rows(v["xa"], v["pa"], rs_a.last())
-    s_a = seq_scatter(v["xa"], v["xsa"], "sa")
     norm1_back(1)
     s_w.wait_recv()
     f[pl.ds(64, 32), :] = jnp.sum(v["xs"][1].astype(F32), axis=0)
@@ -938,7 +1007,8 @@
         scratch_shapes=[
             *SCRATCH.values(),
             *SMALL.values(),
-            *scatter_scratch(ROWS_A, CUT_A, 128),
+            pltpu.VMEM((8, ROWS_A, 128), BF),
+            pltpu.VMEM((7, ROWS_A, 128), BF),
             *scatter_scratch(U1, 48, 768),
             *scatter_scratch(U2, 80, 768),
             *scatter_scratch(ROWS_W, CUT_W, 768),

time: 159 us -> 155 us (0.975)
  Pallas kernels: 156 us -> 152 us
    pallas_call x1, Pallas kernels: 153 us -> 149 us  [on_device(): pl.pallas_call(layer_kernel, out_shape=(sds((2, 128, 768), BF), sds((2, 1...]
where the time goes in v2:
time: 155 us; the launch traced here: 154 us
  Pallas kernels  152 us (98%)
    pallas_call x1, Pallas kernels, on_device(): pl.pallas_call(layer_kernel, out_shape=(sds((2, 128, 768), BF), sds((2, 1...  149 us

profile of v2, /device:TPU:0, one launch (start us, length us, event | category | flops | bytes accessed | tf_op | source)
XLA Modules:
  0.0 154.4 jit_solution(8755415538788853093)
XLA Ops:
  0.6 149.4 %layer.1 = (bf16[2,128,768]{2,1,0:T(8,128)(2,1)}, f32[2,128,768]{2,1,0:T(8,128)}, f32[96,768]{1,0:T(8,128)}) custom-call(bf16[2,128,768]{2,1,0:T(8,128)(2,1)} %refs_0_.1, f32[6,3,768]{2,1,0:T(4,128)} %refs_1_.1, f32[6]{0:T(128)} %refs_2_.1, f32[6]{0:T(128)} %refs_3_.1, f32[6]{0:T(128)} %refs_4_.1, f32[6]{0:T(128)} %refs_5_.1, ...), custom_call_target="tpu_custom_call" | custom-call | tf_op jit(solution)/shard_map/layer/pallas_call | solution.py:1002
  150.0 3.0 %final.1 = (bf16[2,128,768]{2,1,0:T(8,128)(2,1)}, f32[2,128,768]{2,1,0:T(8,128)}, f32[6,3,768]{2,1,0:T(4,128)}, f32[6,768]{1,0:T(8,128)}, f32[6,3072]{1,0:T(8,12...) custom-call(bf16[2,128,768]{2,1,0:T(8,128)(2,1)} %get-tuple-element.20.out_in, f32[2,128,768]{2,1,0:T(8,128)} %get-tuple-element.21.ig_in, ...), custom_call_target="tpu_custom_call" | custom-call | tf_op jit(solution)/shard_map/final/pallas_call | solution.py:1024
  153.0 1.4 slice_bitcast_fusion

commit v3 on v2

--- a/solution.py
+++ b/solution.py
@@ -965,7 +965,7 @@
         store.wait()
 
 
-def final_kernel(out_in, ig_in, f_in, out_ref, ig_ref, dwq_ref, dwo_ref, dwu_ref, dwd_ref, ln_ref, out_v, ig_v, f_ref, sem):
+def final_kernel(out_in, ig_in, f_in, out_ref, ig_ref, dwq_ref, dwo_ref, dwu_ref, dwd_ref, g1_ref, b1_ref, g2_ref, b2_ref, out_v, ig_v, f_ref, sem):
     loads = [
         pltpu.make_async_copy(src, dst, sem.at[i])
         for i, (src, dst) in enumerate(((f_in, f_ref), (ig_in, ig_v), (out_in, out_v)))
@@ -982,7 +982,8 @@
     for c in range(3):
         for i in range(6):
             dwq_ref[i, pl.ds(c, 1), :] = f_ref[pl.ds(c * 6 + i, 1), :]
-    ln_ref[...] = f_ref[pl.ds(24, 8), :]
+    for p, ref in enumerate((g1_ref, b1_ref, g2_ref, b2_ref)):
+        ref[...] = f_ref[24, pl.ds(0, 128)][p * 32 : p * 32 + 6]
     for j in range(4):
         dwu_ref[:, pl.ds(j * 768, 768)] = f_ref[pl.ds(32 + j * 6, 6), :]
     dwo_ref[...] = f_ref[pl.ds(56, 6), :]
@@ -1025,10 +1026,10 @@
         final_kernel,
         out_shape=(
             sds((2, 128, 768), BF), sds((2, 128, 768), F32), sds((6, 3, 768), F32), sds((6, 768), F32),
-            sds((6, 3072), F32), sds((24, 768), F32), sds((8, 768), F32),
+            sds((6, 3072), F32), sds((24, 768), F32), *[sds((6,), F32)] * 4,
         ),
         in_specs=[HBM] * 3,
-        out_specs=[HBM, HBM] + [VM] * 5,
+        out_specs=[HBM, HBM] + [VM] * 8,
         scratch_shapes=[
             pltpu.VMEM((2, 128, 768), BF),
             pltpu.VMEM((2, 128, 768), F32),
@@ -1037,7 +1038,7 @@
         ],
         name="final",
     )(out, ig, sums)
-    return (*res[:6], *[res[6][0, p * 32 : p * 32 + 6] for p in range(4)])
+    return res
 
 
 def solution(mesh):

time: 155 us -> 154 us (level)
  no operation moved by 1% of the time
where the time goes in v3:
time: 154 us; the launch traced here: 153 us
  Pallas kernels  152 us (99%)
    pallas_call x1, Pallas kernels, on_device(): pl.pallas_call(layer_kernel, out_shape=(sds((2, 128, 768), BF), sds((2, 1...  149 us

profile of v3, /device:TPU:0, one launch (start us, length us, event | category | flops | bytes accessed | tf_op | source)
XLA Modules:
  0.0 153.2 jit_solution(14250776036000760184)
XLA Ops:
  0.6 149.4 %layer.1 = (bf16[2,128,768]{2,1,0:T(8,128)(2,1)}, f32[2,128,768]{2,1,0:T(8,128)}, f32[96,768]{1,0:T(8,128)}) custom-call(bf16[2,128,768]{2,1,0:T(8,128)(2,1)} %refs_0_.1, f32[6,3,768]{2,1,0:T(4,128)} %refs_1_.1, f32[6]{0:T(128)} %refs_2_.1, f32[6]{0:T(128)} %refs_3_.1, f32[6]{0:T(128)} %refs_4_.1, f32[6]{0:T(128)} %refs_5_.1, ...), custom_call_target="tpu_custom_call" | custom-call | tf_op jit(solution)/shard_map/layer/pallas_call | solution.py:1003
  150.0 3.0 %final.1 = (bf16[2,128,768]{2,1,0:T(8,128)(2,1)}, f32[2,128,768]{2,1,0:T(8,128)}, f32[6,3,768]{2,1,0:T(4,128)}, f32[6,768]{1,0:T(8,128)}, f32[6,3072]{1,0:T(8,12...) custom-call(bf16[2,128,768]{2,1,0:T(8,128)(2,1)} %get-tuple-element.13.out_in, ...), custom_call_target="tpu_custom_call" | custom-call | tf_op jit(solution)/shard_map/final/pallas_call | solution.py:1025
